TPU v7x, 32 devices: a whole 2x2x4 slice. The times are simulated.
32 devices in a mesh: expert: 8 (over y, x, core), dp: 4 (over z).
Axes of the slice: x: 2, y: 2, z: 4, core: 2. Of those that a mesh axis runs over, the one named last changes fastest.
Arguments:
- frames_in: bfloat16 [8, 512, 1536], P('expert', 'dp'), may hold values from -6 to 6
- conv_kernel: bfloat16 [31, 1536], replicated, may hold values from -1 to 1
- norm_gain: bfloat16 [1536], replicated, may hold values from 0.099609375 to 1.8984375
- router: bfloat16 [1536, 8], replicated, may hold values from -0.15625 to 0.15625
- w_in: bfloat16 [8, 3072, 1536], P('expert', 'dp'), may hold values from -0.15625 to 0.15625
- w_out: bfloat16 [8, 3072, 1536], P('expert', 'dp'), may hold values from -0.109375 to 0.109375
- routes: int32 [8, 512, 2], P('expert', 'dp'), may hold values from 0 to 7, all different within a row; in each aligned block of 128 rows (0 to 127, 128 to 255, ..., all dimensions but the last counted through in order) at most 36 rows name the same one
Outputs:
- block_output: bfloat16 [8, 512, 1536], P('expert', 'dp')
Inputs may be any that keep to these rules, and one draw needn't show every extreme that they name: `routes`: each frame names 2 different experts. In each aligned block of 128 frames of an utterance (the frames of one device) no expert is named more than 36 times, a bound that some block reaches.
All inputs are finite; a program needn't handle non-finite values.
Results may differ from a plain program's by a relative error of at most 0.007.
Values may be sent and summed in bfloat16 or wider, within the bound.
A program may use at most 64 MiB of HBM per device.

v0:
```python
import jax
import jax.numpy as jnp
from jax import lax
from jax.sharding import PartitionSpec as P


def swapped(value, axis, distance):
    mask = 2**distance
    pairs = [(source, source ^ mask) for source in range(lax.axis_size(axis))]
    return lax.ppermute(value, axis, pairs)


def extended(block, sides, width):
    for axis, dim in sides:
        count = lax.axis_size(axis)
        forward = [(i, i + 1) for i in range(count - 1)]
        backward = [(target, source) for source, target in forward]
        low = lax.ppermute(
            lax.slice_in_dim(block, block.shape[dim] - width, None, axis=dim), axis, forward
        )
        high = lax.ppermute(lax.slice_in_dim(block, 0, width, axis=dim), axis, backward)
        block = jnp.concatenate([low, block, high], axis=dim)
    return block


def expert_block(rows, first_w, second_w, row_bits, bit_count):
    place = lax.axis_index("dp")
    for bit in range(row_bits):
        other = swapped(rows, "dp", bit)
        upper = place >> bit & 1 == 1
        rows = jnp.concatenate(
            [jnp.where(upper, other, rows), jnp.where(upper, rows, other)], axis=0
        )
    stacked = jnp.stack([first_w, second_w])
    for bit in range(row_bits, bit_count):
        other = swapped(stacked, "dp", bit)
        stacked = jnp.concatenate([stacked, other], axis=1)
    preact = lax.dot_general(
        rows, stacked[0], (((1,), (1,)), ((), ())), preferred_element_type=jnp.float32
    )
    hidden = jax.nn.silu(preact).astype(jnp.bfloat16)
    partial_value = jnp.dot(hidden, stacked[1], preferred_element_type=jnp.float32)
    for bit in reversed(range(row_bits)):
        half_rows = partial_value.shape[0] // 2
        first_half = partial_value[:half_rows]
        second_half = partial_value[half_rows:]
        upper = place >> bit & 1 == 1
        outgoing = jnp.where(upper, first_half, second_half)
        kept = jnp.where(upper, second_half, first_half)
        partial_value = kept + swapped(outgoing.astype(jnp.bfloat16), "dp", bit).astype(
            outgoing.dtype
        )
    return partial_value


def shards(frames_in, conv_kernel, norm_gain, router, w_in, w_out, routes):
    tok_rows = frames_in.shape[1]
    features = frames_in.shape[2]
    kernel_len = conv_kernel.shape[0]
    margin = (kernel_len - 1) // 2
    padded = extended(frames_in, (("dp", 1),), margin)
    frames_f = frames_in[0].astype(jnp.float32)
    convolved = jnp.zeros((tok_rows, features), jnp.float32)
    for offset in range(kernel_len):
        convolved = convolved + conv_kernel[offset].astype(jnp.float32) * padded[
            0, offset : offset + tok_rows
        ].astype(jnp.float32)
    residual = frames_f + jax.nn.silu(convolved)
    scale_rms = lax.rsqrt(jnp.mean(residual * residual, axis=-1, keepdims=True) + 1e-06)
    normed = (residual * scale_rms * norm_gain.astype(jnp.float32)).astype(jnp.bfloat16)
    logits = jnp.dot(normed, router, preferred_element_type=jnp.float32)
    expert_count = router.shape[1]
    chosen = routes[0]
    top_k = chosen.shape[1]
    onehot = (chosen[:, :, None] == jnp.arange(expert_count, dtype=jnp.int32)).astype(jnp.float32)
    gating = jax.nn.sigmoid(jnp.sum(onehot * logits[:, None, :], axis=-1))
    pair_count = tok_rows * top_k
    flat_hot = onehot.reshape(pair_count, expert_count)
    positions = jnp.arange(pair_count, dtype=jnp.int32)
    earlier = (positions[:, None] > positions[None, :]).astype(jnp.float32)
    counts = jnp.dot(earlier, flat_hot, precision=lax.Precision.HIGHEST)
    slot_of = jnp.sum(counts * flat_hot, axis=-1).astype(jnp.int32)
    capacity = max(2, 9 * top_k * tok_rows // (8 * lax.axis_size("expert")))
    target = chosen.reshape(pair_count) * capacity + slot_of
    placing = (
        jnp.arange(expert_count * capacity, dtype=jnp.int32)[:, None] == target[None, :]
    ).astype(jnp.bfloat16)
    normed_rep = jnp.repeat(normed, top_k, axis=0)
    sent_normed = (
        jnp.dot(placing, normed_rep, preferred_element_type=jnp.float32)
        .astype(jnp.bfloat16)
        .reshape(expert_count, capacity, features)
    )
    received = lax.all_to_all(sent_normed, "expert", split_axis=0, concat_axis=0, tiled=True)
    slot_block = received.reshape(expert_count * capacity, features)
    bit_count = lax.axis_size("dp").bit_length() - 1
    row_bits = bit_count // 2
    summed = expert_block(slot_block, w_in[0], w_out[0], row_bits, bit_count)
    expert_out = summed.astype(jnp.bfloat16).reshape(expert_count, capacity, features)
    returned = lax.all_to_all(
        expert_out, "expert", split_axis=0, concat_axis=0, tiled=True
    ).reshape(expert_count * capacity, features)
    pulled_back = lax.dot_general(
        placing, returned, (((0,), (0,)), ((), ())), preferred_element_type=jnp.float32
    )
    pulled_back = pulled_back.reshape(tok_rows, top_k, features)
    combined = (residual + jnp.sum(gating[:, :, None] * pulled_back, axis=1)).astype(jnp.bfloat16)
    return combined[None]


def solution(mesh):
    return jax.shard_map(
        shards,
        mesh=mesh,
        in_specs=(
            P("expert", "dp", None),
            P(),
            P(),
            P(),
            P("expert", "dp", None),
            P("expert", "dp", None),
            P("expert", "dp", None),
        ),
        out_specs=P("expert", "dp", None),
        check_vma=False,
    )
```

profile of v0, /device:TPU:29, one launch (start us, length us, event | category | flops | bytes accessed | tf_op | source)
XLA Modules:
  0.0 278.4 jit_solution(9208277500844189814)
XLA Ops:
  0.0 1.0 fusion.134
  1.0 1.3 collective-permute-start
  2.3 0.0 copy-start.1
  2.3 4.1 %collective-permute-start.1 = (bf16[1,15,1536]{2,1,0:T(8,128)(2,1)S(1)}, bf16[1,15,1536]{2,1,0:T(8,128)(2,1)S(1)}, u32[]{:S(2)}, u32[]{:S(2)}) collective-permute-start(bf16[1,15,1536]{2,1,0:T(8,128)(2,1)S(1)} %get-tuple-element.41), channel_id=1, source_target_pairs={{1,0},{2,1},{3,2},{5,4},{6,5},{7,6},{9,8},{10,9},{11,10},{13,12},{... | collective-permute-start | bytes 138248 | tf_op jit(solution)/shard_map/ppermute | solution.py:21
  6.4 3.3 %constant_dynamic-update-slice_fusion.3 = bf16[2,768,1536]{2,1,0:T(8,128)(2,1)} fusion(bf16[1,768,1536]{2,1,0:T(8,128)(2,1)} %param.11), kind=kLoop, calls=%fused_computation.218 | loop fusion | bytes 4718592
  9.7 1.6 constant_dynamic-update-slice_fusion.2
  11.3 0.1 collective-permute-start.3
  11.4 0.0 copy-done.36
  11.4 0.1 copy.14
  11.5 0.1 reshape_squeeze.3
  11.7 0.2 fusion.18
  11.9 0.3 convert_reduce_fusion.30
  12.2 0.0 copy-start.4
  12.3 0.2 convert_reduce_fusion.29
  12.5 0.0 copy-done.37
  12.5 0.0 copy-start.20
  12.6 0.0 copy-start.22
  12.6 0.0 copy-start.24
  12.6 0.0 copy-start.26
  12.6 0.0 copy-start.28
  12.7 0.0 collective-permute-done.1
  12.7 0.0 collective-permute-done
  12.7 4.0 %multiply_reduce_fusion = (f32[128]{0:T(128)S(1)}, f32[128,1536]{1,0:T(8,128)S(1)}) fusion(bf16[1,143,1536]{2,1,0:T(8,128)(2,1)S(1)} %constant_dynamic-update-slice_fusion, f32[1536]{0:T(1024)S(1)} %get-tuple-element.34, f32[1536]{0:T(1024)S(1)} %get-tuple-element.35, f32[1536]{0:T(1024)S(1)} %get-tuple-element.6, f32[1536]{0:T(1024)S(1)} %get-tuple-element.7, ...), kind=kLoop, calls=%fused_computation.194 | loop fusion | flops 28311424 | bytes 7314944 | tf_op jit(solution)/shard_map/reduce_sum | solution.py:69
  16.9 0.1 multiply_convert_fusion.1
  17.0 0.4 broadcast_in_dim.2
  17.4 0.3 reshape.352
  17.7 0.4 convolution_convert_fusion
  18.1 0.2 reshape.353
  18.3 17.8 %all_to_all.10 = bf16[8,36,1536]{2,1,0:T(8,128)(2,1)S(1)} all-to-all(bf16[8,36,1536]{2,1,0:T(8,128)(2,1)S(1)} %reshape.353), channel_id=1, replica_groups=mesh['expert'=8,'dp'=4] {'expert'}, dimensions={0} | all-to-all | bytes 1769472 | tf_op jit(solution)/shard_map/all_to_all | solution.py:94
  36.1 0.2 reshape.354
  36.3 0.1 collective-permute-start.2
  36.3 94.2 %collective-permute-done.2 = bf16[288,1536]{1,0:T(8,128)(2,1)S(1)} collective-permute-done((bf16[288,1536]{1,0:T(8,128)(2,1)S(1)}, bf16[288,1536]{1,0:T(8,128)(2,1)S(1)}, u32[]{:S(2)}, u32[]{:S(2)}) %collective-permute-start.2) | collective-permute-done | bytes 884768 | tf_op jit(solution)/shard_map/ppermute | solution.py:10
  130.5 1.3 broadcast_select_fusion.1
  131.8 85.4 %collective-permute-done.3 = bf16[2,768,1536]{2,1,0:T(8,128)(2,1)} collective-permute-done((bf16[2,768,1536]{2,1,0:T(8,128)(2,1)}, bf16[2,768,1536]{2,1,0:T(8,128)(2,1)}, u32[]{:S(2)}, u32[]{:S(2)}) %collective-permute-start.3) | collective-permute-done | bytes 4718624 | tf_op jit(solution)/shard_map/ppermute | solution.py:10
  217.3 12.0 %fusion.5 = f32[576,1536]{1,0:T(8,128)} fusion(bf16[2,768,1536]{2,1,0:T(8,128)(2,1)} %collective-permute-done.3, bf16[2,768,1536]{2,1,0:T(8,128)(2,1)} %constant_dynamic-update-slice_fusion.2, bf16[288,1536]{1,0:T(8,128)(2,1)} %get-tuple-element.39, bf16[288,1536]{1,0:T(8,128)(2,1)} %get-tuple-element.38), kind=kOutput, calls=%fused_computation.7 | convolution fusion | flops 5462654976 | bytes 24182784 | tf_op jit(solution)/shard_map/dot_general | solution.py:42
  229.3 2.2 select_convert_fusion
  231.5 0.1 collective-permute-start.4
  231.6 20.7 %collective-permute-done.4 = bf16[288,1536]{1,0:T(8,128)(2,1)S(1)} collective-permute-done((bf16[288,1536]{1,0:T(8,128)(2,1)S(1)}, bf16[288,1536]{1,0:T(8,128)(2,1)S(1)}, u32[]{:S(2)}, u32[]{:S(2)}) %collective-permute-start.4) | collective-permute-done | bytes 884768 | tf_op jit(solution)/shard_map/ppermute | solution.py:10
  252.3 2.5 add_convert_fusion
  254.8 1.1 reshape.355
  256.0 5.4 %all-to-all-start.1 = ((bf16[8,36,1536]{2,1,0:T(8,128)(2,1)}), bf16[8,36,1536]{2,1,0:T(8,128)(2,1)S(1)}, u32[]{:S(2)}, u32[]{:S(2)}) async-start(bf16[8,36,1536]{2,1,0:T(8,128)(2,1)} %reshape.355), calls=%async_computation.1 | async-start | bytes 1966080 | tf_op jit(solution)/shard_map/all_to_all | solution.py:100
  261.3 0.1 iota_compare_fusion
  261.5 0.1 eq.65
  261.6 0.2 fusion.135
  261.8 10.4 %all-to-all-done.1 = bf16[8,36,1536]{2,1,0:T(8,128)(2,1)S(1)} async-done(((bf16[8,36,1536]{2,1,0:T(8,128)(2,1)}), bf16[8,36,1536]{2,1,0:T(8,128)(2,1)S(1)}, u32[]{:S(2)}, u32[]{:S(2)}) %all-to-all-start.1) | async-done | bytes 884768 | tf_op jit(solution)/shard_map/all_to_all | solution.py:100
  272.3 0.2 reshape.419
  272.5 0.6 fusion.13
  273.2 5.2 %fusion.112 = bf16[1,128,1536]{2,1,0:T(8,128)(2,1)} fusion(bf16[1,128,1536]{2,1,0:T(8,128)(2,1)S(1)} %copy-done.1, f32[128,1536]{1,0:T(8,128)S(1)} %fusion.13, bf16[1,15,1536]{2,1,0:T(8,128)(2,1)S(1)} %collective-permute-done, f32[1536]{0:T(1024)} %copy-done.34, f32[1536]{0:T(1024)} %copy-done.35, f32[1536]{0:T(1024)S(1)} %get-tuple-element.6, ...), kind=kLoop, calls=%fused_computation.192 | loop fusion | flops 28311552 | bytes 7707648 | tf_op jit(solution)/shard_map/convert_element_type | solution.py:107
  (74 shorter events, 0.2 us)
Async XLA Ops:
  0.0 261.6 %copy-start = (bf16[1536,8]{0,1:T(8,128)(2,1)S(1)}, bf16[1536,8]{0,1:T(8,128)(2,1)}, u32[]{:S(2)}) copy-start(bf16[1536,8]{0,1:T(8,128)(2,1)} %param.10) | copy-start | bytes 73732
  0.0 9.7 %copy-start.2 = (bf16[1,768,1536]{2,1,0:T(8,128)(2,1)S(1)}, bf16[1,768,1536]{2,1,0:T(8,128)(2,1)}, u32[]{:S(2)}) copy-start(bf16[1,768,1536]{2,1,0:T(8,128)(2,1)} %param.12) | copy-start | bytes 7077892
  1.0 11.7 %collective-permute-start = (bf16[1,15,1536]{2,1,0:T(8,128)(2,1)S(1)}, bf16[1,15,1536]{2,1,0:T(8,128)(2,1)S(1)}, u32[]{:S(2)}, u32[]{:S(2)}) collective-permute-start(bf16[1,15,1536]{2,1,0:T(8,128)(2,1)S(1)} %get-tuple-element.40), channel_id=1, source_target_pairs={{0,1},{1,2},{2,3},{4,5},{5,6},{6,7},{8,9},{9,10},{10,11},{12,13},{... | collective-permute-start | bytes 138248 | tf_op jit(solution)/shard_map/ppermute | solution.py:18
  2.3 9.1 %copy-start.1 = (bf16[1,128,1536]{2,1,0:T(8,128)(2,1)S(1)}, bf16[1,128,1536]{2,1,0:T(8,128)(2,1)}, u32[]{:S(2)}) copy-start(bf16[1,128,1536]{2,1,0:T(8,128)(2,1)} %param.7) | copy-start | bytes 1179652
  2.3 10.4 %collective-permute-start.1 = (bf16[1,15,1536]{2,1,0:T(8,128)(2,1)S(1)}, bf16[1,15,1536]{2,1,0:T(8,128)(2,1)S(1)}, u32[]{:S(2)}, u32[]{:S(2)}) collective-permute-start(bf16[1,15,1536]{2,1,0:T(8,128)(2,1)S(1)} %get-tuple-element.41), channel_id=1, source_target_pairs={{1,0},{2,1},{3,2},{5,4},{6,5},{7,6},{9,8},{10,9},{11,10},{13,12},{... | collective-permute-start | bytes 138248 | tf_op jit(solution)/shard_map/ppermute | solution.py:21
  9.7 1.7 copy-start.36
  9.7 2.2 copy-start.3
  9.7 2.8 %copy-start.37 = (bf16[1536]{0:T(1024)(128)(2,1)S(1)}, bf16[1536]{0:T(1024)(128)(2,1)}, u32[]{:S(2)}) copy-start(bf16[1536]{0:T(1024)(128)(2,1)} %param.9) | copy-start | bytes 9220
  11.3 205.9 %collective-permute-start.3 = (bf16[2,768,1536]{2,1,0:T(8,128)(2,1)}, bf16[2,768,1536]{2,1,0:T(8,128)(2,1)}, u32[]{:S(2)}, u32[]{:S(2)}) collective-permute-start(bf16[2,768,1536]{2,1,0:T(8,128)(2,1)} %constant_dynamic-update-slice_fusion.2), channel_id=1, source_target_pairs={{0,2},{1,3},{2,0},{3,1},{4,6},{5,7},{6,4},{7,5},{8,10},{9,11},{10,... | collective-permute-start | bytes 14155784 | tf_op jit(solution)/shard_map/ppermute | solution.py:10
  12.2 4.4 %copy-start.4 = (f32[1536]{0:T(1024)}, f32[1536]{0:T(1024)S(1)}, u32[]{:S(2)}) copy-start(f32[1536]{0:T(1024)S(1)} %get-tuple-element.16) | copy-start | bytes 18436
  12.2 4.4 %copy-start.6 = (f32[1536]{0:T(1024)}, f32[1536]{0:T(1024)S(1)}, u32[]{:S(2)}) copy-start(f32[1536]{0:T(1024)S(1)} %get-tuple-element.17) | copy-start | bytes 18436
  12.3 4.4 %copy-start.8 = (f32[1536]{0:T(1024)}, f32[1536]{0:T(1024)S(1)}, u32[]{:S(2)}) copy-start(f32[1536]{0:T(1024)S(1)} %get-tuple-element.18) | copy-start | bytes 18436
  12.3 4.4 %copy-start.10 = (f32[1536]{0:T(1024)}, f32[1536]{0:T(1024)S(1)}, u32[]{:S(2)}) copy-start(f32[1536]{0:T(1024)S(1)} %get-tuple-element.19) | copy-start | bytes 18436
  12.3 4.4 %copy-start.12 = (f32[1536]{0:T(1024)}, f32[1536]{0:T(1024)S(1)}, u32[]{:S(2)}) copy-start(f32[1536]{0:T(1024)S(1)} %get-tuple-element.20) | copy-start | bytes 18436
  12.3 4.4 %copy-start.14 = (f32[1536]{0:T(1024)}, f32[1536]{0:T(1024)S(1)}, u32[]{:S(2)}) copy-start(f32[1536]{0:T(1024)S(1)} %get-tuple-element.21) | copy-start | bytes 18436
  12.3 4.4 %copy-start.16 = (f32[1536]{0:T(1024)}, f32[1536]{0:T(1024)S(1)}, u32[]{:S(2)}) copy-start(f32[1536]{0:T(1024)S(1)} %get-tuple-element.22) | copy-start | bytes 18436
  12.3 4.4 %copy-start.18 = (f32[1536]{0:T(1024)}, f32[1536]{0:T(1024)S(1)}, u32[]{:S(2)}) copy-start(f32[1536]{0:T(1024)S(1)} %get-tuple-element.23) | copy-start | bytes 18436
  12.5 4.2 %copy-start.20 = (f32[1536]{0:T(1024)}, f32[1536]{0:T(1024)S(1)}, u32[]{:S(2)}) copy-start(f32[1536]{0:T(1024)S(1)} %get-tuple-element.24) | copy-start | bytes 18436
  12.6 4.2 %copy-start.22 = (f32[1536]{0:T(1024)}, f32[1536]{0:T(1024)S(1)}, u32[]{:S(2)}) copy-start(f32[1536]{0:T(1024)S(1)} %get-tuple-element.25) | copy-start | bytes 18436
  12.6 4.2 %copy-start.24 = (f32[1536]{0:T(1024)}, f32[1536]{0:T(1024)S(1)}, u32[]{:S(2)}) copy-start(f32[1536]{0:T(1024)S(1)} %get-tuple-element.26) | copy-start | bytes 18436
  12.6 4.2 %copy-start.26 = (f32[1536]{0:T(1024)}, f32[1536]{0:T(1024)S(1)}, u32[]{:S(2)}) copy-start(f32[1536]{0:T(1024)S(1)} %get-tuple-element.27) | copy-start | bytes 18436
  12.6 4.2 %copy-start.28 = (f32[1536]{0:T(1024)}, f32[1536]{0:T(1024)S(1)}, u32[]{:S(2)}) copy-start(f32[1536]{0:T(1024)S(1)} %get-tuple-element.28) | copy-start | bytes 18436
  12.6 4.2 %copy-start.29 = (f32[1536]{0:T(1024)}, f32[1536]{0:T(1024)S(1)}, u32[]{:S(2)}) copy-start(f32[1536]{0:T(1024)S(1)} %get-tuple-element.29) | copy-start | bytes 18436
  12.6 4.2 %copy-start.30 = (f32[1536]{0:T(1024)}, f32[1536]{0:T(1024)S(1)}, u32[]{:S(2)}) copy-start(f32[1536]{0:T(1024)S(1)} %get-tuple-element.30) | copy-start | bytes 18436
  12.6 4.2 %copy-start.31 = (f32[1536]{0:T(1024)}, f32[1536]{0:T(1024)S(1)}, u32[]{:S(2)}) copy-start(f32[1536]{0:T(1024)S(1)} %get-tuple-element.31) | copy-start | bytes 18436
  12.6 4.2 %copy-start.32 = (f32[1536]{0:T(1024)}, f32[1536]{0:T(1024)S(1)}, u32[]{:S(2)}) copy-start(f32[1536]{0:T(1024)S(1)} %get-tuple-element.32) | copy-start | bytes 18436
  12.6 4.2 %copy-start.33 = (f32[1536]{0:T(1024)}, f32[1536]{0:T(1024)S(1)}, u32[]{:S(2)}) copy-start(f32[1536]{0:T(1024)S(1)} %get-tuple-element.33) | copy-start | bytes 18436
  12.6 4.2 %copy-start.34 = (f32[1536]{0:T(1024)}, f32[1536]{0:T(1024)S(1)}, u32[]{:S(2)}) copy-start(f32[1536]{0:T(1024)S(1)} %get-tuple-element.34) | copy-start | bytes 18436
  12.7 4.2 %copy-start.35 = (f32[1536]{0:T(1024)}, f32[1536]{0:T(1024)S(1)}, u32[]{:S(2)}) copy-start(f32[1536]{0:T(1024)S(1)} %get-tuple-element.35) | copy-start | bytes 18436
  36.3 94.2 %collective-permute-start.2 = (bf16[288,1536]{1,0:T(8,128)(2,1)S(1)}, bf16[288,1536]{1,0:T(8,128)(2,1)S(1)}, u32[]{:S(2)}, u32[]{:S(2)}) collective-permute-start(bf16[288,1536]{1,0:T(8,128)(2,1)S(1)} %reshape.354), channel_id=1, source_target_pairs={{0,1},{1,0},{2,3},{3,2},{4,5},{5,4},{6,7},{7,6},{8,9},{9,8},{10,11... | collective-permute-start | bytes 2654216 | tf_op jit(solution)/shard_map/ppermute | solution.py:10
  231.5 20.8 %collective-permute-start.4 = (bf16[288,1536]{1,0:T(8,128)(2,1)S(1)}, bf16[288,1536]{1,0:T(8,128)(2,1)S(1)}, u32[]{:S(2)}, u32[]{:S(2)}) collective-permute-start(bf16[288,1536]{1,0:T(8,128)(2,1)S(1)} %select_convert_fusion), channel_id=1, source_target_pairs={{0,1},{1,0},{2,3},{3,2},{4,5},{5,4},{6,7},{7,6},{8,9},{9,8},{10,11... | collective-permute-start | bytes 2654216 | tf_op jit(solution)/shard_map/ppermute | solution.py:10
  255.9 17.2 %copy-start.5 = (f32[1536]{0:T(1024)S(1)}, f32[1536]{0:T(1024)}, u32[]{:S(2)}) copy-start(f32[1536]{0:T(1024)} %copy-done.4) | copy-start | bytes 18436
  255.9 17.2 %copy-start.7 = (f32[1536]{0:T(1024)S(1)}, f32[1536]{0:T(1024)}, u32[]{:S(2)}) copy-start(f32[1536]{0:T(1024)} %copy-done.6) | copy-start | bytes 18436
  255.9 17.2 %copy-start.9 = (f32[1536]{0:T(1024)S(1)}, f32[1536]{0:T(1024)}, u32[]{:S(2)}) copy-start(f32[1536]{0:T(1024)} %copy-done.8) | copy-start | bytes 18436
  255.9 17.2 %copy-start.11 = (f32[1536]{0:T(1024)S(1)}, f32[1536]{0:T(1024)}, u32[]{:S(2)}) copy-start(f32[1536]{0:T(1024)} %copy-done.10) | copy-start | bytes 18436
  255.9 17.2 %copy-start.13 = (f32[1536]{0:T(1024)S(1)}, f32[1536]{0:T(1024)}, u32[]{:S(2)}) copy-start(f32[1536]{0:T(1024)} %copy-done.12) | copy-start | bytes 18436
  255.9 17.2 %copy-start.15 = (f32[1536]{0:T(1024)S(1)}, f32[1536]{0:T(1024)}, u32[]{:S(2)}) copy-start(f32[1536]{0:T(1024)} %copy-done.14) | copy-start | bytes 18436
  255.9 17.2 %copy-start.17 = (f32[1536]{0:T(1024)S(1)}, f32[1536]{0:T(1024)}, u32[]{:S(2)}) copy-start(f32[1536]{0:T(1024)} %copy-done.16) | copy-start | bytes 18436
  255.9 17.2 %copy-start.19 = (f32[1536]{0:T(1024)S(1)}, f32[1536]{0:T(1024)}, u32[]{:S(2)}) copy-start(f32[1536]{0:T(1024)} %copy-done.18) | copy-start | bytes 18436
  255.9 17.2 %copy-start.21 = (f32[1536]{0:T(1024)S(1)}, f32[1536]{0:T(1024)}, u32[]{:S(2)}) copy-start(f32[1536]{0:T(1024)} %copy-done.20) | copy-start | bytes 18436
  255.9 17.2 %copy-start.23 = (f32[1536]{0:T(1024)S(1)}, f32[1536]{0:T(1024)}, u32[]{:S(2)}) copy-start(f32[1536]{0:T(1024)} %copy-done.22) | copy-start | bytes 18436
  256.0 17.2 %copy-start.25 = (f32[1536]{0:T(1024)S(1)}, f32[1536]{0:T(1024)}, u32[]{:S(2)}) copy-start(f32[1536]{0:T(1024)} %copy-done.24) | copy-start | bytes 18436
  256.0 17.2 %copy-start.27 = (f32[1536]{0:T(1024)S(1)}, f32[1536]{0:T(1024)}, u32[]{:S(2)}) copy-start(f32[1536]{0:T(1024)} %copy-done.26) | copy-start | bytes 18436
  256.0 16.3 %all-to-all-start.1 = ((bf16[8,36,1536]{2,1,0:T(8,128)(2,1)}), bf16[8,36,1536]{2,1,0:T(8,128)(2,1)S(1)}, u32[]{:S(2)}, u32[]{:S(2)}) async-start(bf16[8,36,1536]{2,1,0:T(8,128)(2,1)} %reshape.355), calls=%async_computation.1 | async-start | bytes 1966080 | tf_op jit(solution)/shard_map/all_to_all | solution.py:100
where the time goes:
time: 282 us; the launch traced here: 278 us
  waiting for transfers between devices  211 us (75%)
  blocking collectives  17.8 us (6%)
  other arithmetic  16 us (6%)
  matrix products  13.4 us (5%)
  starting transfers between devices  11 us (4%)
  local copies, waits for them, and re-layouts  8.78 us (3%)
    ppermute x3, waiting for transfers between devices, swapped(): return lax.ppermute(value, axis, pairs)  200 us
    all_to_all x1, blocking collectives, shards(): lax.all_to_all(sent_normed, 'expert', split_axis=0, concat_axis=0, tiled=...  17.8 us
    dot_general x1, matrix products, expert_block(): jnp.dot(hidden, stacked[1], preferred_element_type=jnp.float32)  12 us
    all_to_all x1, waiting for transfers between devices, shards(): lax.all_to_all(expert_out, 'expert', split_axis=0, concat_axis=0, tiled=T...  10.4 us
  transfers between devices with their start and end apart: 6, of which 4 were waited for; matrix products, arithmetic and copies ran while one was open for 5% of the time, Pallas kernels for 0%

commit v1 on v0

--- a/solution.py
+++ b/solution.py
@@ -1,6 +1,10 @@
+import functools
+
 import jax
 import jax.numpy as jnp
 from jax import lax
+from jax.experimental import pallas as pl
+from jax.experimental.pallas import tpu as pltpu
 from jax.sharding import PartitionSpec as P
 
 
@@ -108,9 +112,445 @@
     return combined[None]
 
 
+COL = 256
+LANE = 128
+HALO = 16
+BF = jnp.bfloat16
+F32 = jnp.float32
+MESH = pl.DeviceIdType.MESH
+
+
+def silu(v):
+    return v / (1.0 + jnp.exp(-v))
+
+
+def moe_kernel(
+    n_ex, n_dp, cap,
+    x_ref, ck_ref, gain_ref, rout_ref, routes_ref, w_in_ref, w_out_ref,
+    o_ref,
+    xp, xf, res, info, place, gate, frames, rows_out, rows_in, acc, hid, part_out, part_in,
+    comb_out, comb_in, w1, w2, logit,
+    w1_sem, w2_sem, halo_s, halo_r, info_s, info_r, zs, zr, xs, xr, ys, yr, rs, rr,
+):
+    tok, width = x_ref.shape[1], x_ref.shape[2]
+    ff = w_in_ref.shape[1]
+    cols = width // COL
+    ffb = ff // COL
+    margin = (ck_ref.shape[0] - 1) // 2
+    seg = n_dp * cap
+    slots = n_ex * seg
+    ex = lax.axis_index("expert")
+    dp = lax.axis_index("dp")
+    blk = slots // 4
+
+    def dp_peer(d):
+        return lax.rem(dp + d, n_dp)
+
+    def ex_peer(d):
+        return lax.rem(ex + d, n_ex)
+
+    def rem_copy(src, dst, ssem, rsem, e, v):
+        return pltpu.make_async_remote_copy(
+            src_ref=src, dst_ref=dst, send_sem=ssem, recv_sem=rsem,
+            device_id=(e, v), device_id_type=MESH,
+        )
+
+    barrier = pltpu.get_barrier_semaphore()
+    for d in range(1, n_dp):
+        pl.semaphore_signal(barrier, inc=1, device_id=(ex, dp_peer(d)), device_id_type=MESH)
+    for d in range(1, n_ex):
+        pl.semaphore_signal(barrier, inc=1, device_id=(ex_peer(d), dp), device_id_type=MESH)
+
+    def w1_copy(k):
+        return pltpu.make_async_copy(
+            w_in_ref.at[0, :, pl.ds(k * COL, COL)], w1.at[k], w1_sem.at[k]
+        )
+
+    def w2_copy(k):
+        return pltpu.make_async_copy(
+            w_out_ref.at[0, :, pl.ds(k * COL, COL)], w2.at[k], w2_sem.at[k]
+        )
+
+    for k in range(cols):
+        w1_copy(k).start()
+        w2_copy(k).start()
+
+    xp[HALO : HALO + tok, :] = x_ref[0]
+    expert_of = lax.broadcasted_iota(jnp.int32, (n_ex, tok), 0)
+    hot = [(expert_of == routes_ref[k : k + 1, :]).astype(F32) for k in range(2)]
+    before = (
+        lax.broadcasted_iota(jnp.int32, (tok, tok), 0)
+        < lax.broadcasted_iota(jnp.int32, (tok, tok), 1)
+    ).astype(BF)
+    count = jnp.dot((hot[0] + hot[1]).astype(BF), before, preferred_element_type=F32)
+    counts = [count, count + hot[0]]
+    rows8 = lax.broadcasted_iota(jnp.int32, (8, tok), 0)
+    targets = [
+        routes_ref[k : k + 1, :].astype(F32) * seg
+        + (dp * cap).astype(F32)
+        + jnp.sum(counts[k] * hot[k], axis=0, keepdims=True)
+        for k in range(2)
+    ]
+    info[0, dp] = jnp.where(rows8 == 0, targets[0], targets[1])
+
+    pl.semaphore_wait(barrier, n_dp - 1 + n_ex - 1)
+
+    def up_copy():
+        return rem_copy(
+            x_ref.at[0, pl.ds(tok - HALO, HALO)], xp.at[pl.ds(0, HALO)],
+            halo_s.at[0], halo_r.at[0], ex, dp_peer(1),
+        )
+
+    def down_copy():
+        return rem_copy(
+            x_ref.at[0, pl.ds(0, HALO)], xp.at[pl.ds(HALO + tok, HALO)],
+            halo_s.at[1], halo_r.at[1], ex, dp_peer(n_dp - 1),
+        )
+
+    @pl.when(dp < n_dp - 1)
+    def _():
+        up_copy().start()
+
+    @pl.when(dp > 0)
+    def _():
+        down_copy().start()
+
+    def info_copy(i, d, src):
+        return rem_copy(
+            info.at[i, src], info.at[i, src], info_s.at[i, d], info_r.at[i, d], ex, dp_peer(d)
+        )
+
+    for d in range(1, n_dp):
+        info_copy(0, d, dp).start()
+
+    @pl.when(dp == 0)
+    def _():
+        xp[0:HALO, :] = jnp.zeros((HALO, width), BF)
+
+    @pl.when(dp == n_dp - 1)
+    def _():
+        xp[HALO + tok :, :] = jnp.zeros((HALO, width), BF)
+
+    @pl.when(dp > 0)
+    def _():
+        up_copy().wait_recv()
+
+    @pl.when(dp < n_dp - 1)
+    def _():
+        down_copy().wait_recv()
+
+    def conv_step(c, total):
+        at = pl.ds(pl.multiple_of(c * LANE, LANE), LANE)
+        xf[...] = xp[:, at].astype(F32)
+        taps = ck_ref[:, at].astype(F32)
+        conv = jnp.zeros((tok, LANE), F32)
+        for j in range(ck_ref.shape[0]):
+            first = HALO - margin + j
+            conv = conv + taps[j : j + 1, :] * xf[first : first + tok, :]
+        value = xf[HALO : HALO + tok, :] + silu(conv)
+        res[:, at] = value
+        return total + jnp.sum(value * value, axis=1, keepdims=True)
+
+    total = lax.fori_loop(0, width // LANE, conv_step, jnp.zeros((tok, 1), F32))
+    scale = lax.rsqrt(total * (1.0 / width) + 1e-6)
+
+    own = pl.ds(pl.multiple_of(dp * tok, tok), tok)
+
+    def z_copy(k, d):
+        return rem_copy(
+            frames.at[k, own], frames.at[k, own], zs.at[k, d], zr.at[k, d], ex, dp_peer(d)
+        )
+
+    logit[...] = jnp.zeros_like(logit)
+
+    def norm_step(k, carry):
+        at = pl.ds(pl.multiple_of(k * COL, COL), COL)
+        normed = (res[:, at] * scale * gain_ref[:, at].astype(F32)).astype(BF)
+        frames[k, own] = normed
+        for d in range(1, n_dp):
+            z_copy(k, d).start()
+        logit[...] += lax.dot_general(
+            rout_ref[:, at], normed, (((1,), (1,)), ((), ())), preferred_element_type=F32
+        )
+        return carry
+
+    lax.fori_loop(0, cols, norm_step, 0)
+    gating = [
+        1.0 / (1.0 + jnp.exp(-jnp.sum(hot[k] * logit[...], axis=0, keepdims=True)))
+        for k in range(2)
+    ]
+    info[1, dp] = jnp.where(rows8 == 0, gating[0], gating[1])
+    for d in range(1, n_dp):
+        info_copy(1, d, dp).start()
+    for d in range(1, n_dp):
+        info_copy(0, d, dp).wait_recv()
+
+    def place_step(b, carry):
+        at = pl.ds(pl.multiple_of(b * blk, 16), blk)
+        index = (lax.broadcasted_iota(jnp.int32, (blk, tok), 0) + b * blk).astype(F32)
+        for v in range(n_dp):
+            first, second = info[0, v, 0:1, :], info[0, v, 1:2, :]
+            hits = jnp.where(index == first, 1.0, 0.0) + jnp.where(index == second, 1.0, 0.0)
+            place[at, v * tok : (v + 1) * tok] = hits.astype(BF)
+        return carry
+
+    lax.fori_loop(0, 4, place_step, 0)
+
+    mine_seg = pl.ds(pl.multiple_of(ex * seg, 16), seg)
+
+    def seg_of(e):
+        return pl.ds(pl.multiple_of(e * seg, 16), seg)
+
+    def x_copy(k, d):
+        return rem_copy(
+            rows_out.at[k, seg_of(ex_peer(d))], rows_in.at[k, mine_seg],
+            xs.at[k, d], xr.at[k, d], ex_peer(d), dp,
+        )
+
+    def y_copy(k, d):
+        return rem_copy(
+            part_out.at[k, seg_of(ex_peer(d))], part_in.at[k, mine_seg],
+            ys.at[k, d], yr.at[k, d], ex_peer(d), dp,
+        )
+
+    for k in range(cols):
+        w1_copy(k).wait()
+    lag = 2
+
+    def in_step(s, carry):
+        @pl.when(s < cols)
+        def _():
+            for d in range(1, n_dp):
+                z_copy(s, d).wait_recv()
+
+            def rows_step(b, c2):
+                at = pl.ds(pl.multiple_of(b * blk, 16), blk)
+                rows_out[s, at] = jnp.dot(
+                    place[at, :], frames[s], preferred_element_type=F32
+                ).astype(BF)
+                return c2
+
+            lax.fori_loop(0, 4, rows_step, 0)
+            for d in range(1, n_ex):
+                x_copy(s, d).start()
+            rows_in[s, mine_seg] = rows_out[s, mine_seg]
+
+        @pl.when(s >= lag)
+        def _():
+            k = s - lag
+            for d in range(1, n_ex):
+                x_copy(k, d).wait_recv()
+
+            def ff_step(n, c2):
+                at = pl.ds(pl.multiple_of(n * COL, COL), COL)
+                got = lax.dot_general(
+                    rows_in[k], w1[k, at], (((1,), (1,)), ((), ())), preferred_element_type=F32
+                )
+
+                @pl.when(k == 0)
+                def _():
+                    acc[n] = got
+
+                @pl.when(k > 0)
+                def _():
+                    acc[n] += got
+
+                return c2
+
+            lax.fori_loop(0, ffb, ff_step, 0)
+
+        return carry
+
+    lax.fori_loop(0, cols + lag, in_step, 0)
+
+    def silu_step(b, carry):
+        at = pl.ds(pl.multiple_of(b * blk, 16), blk)
+        for n in range(ffb):
+            hid[n, at] = silu(acc[n, at]).astype(BF)
+        return carry
+
+    lax.fori_loop(0, 4, silu_step, 0)
+
+    for d in range(1, n_dp):
+        info_copy(1, d, dp).wait_recv()
+    eye = (
+        lax.broadcasted_iota(jnp.int32, (tok, tok), 0)
+        == lax.broadcasted_iota(jnp.int32, (tok, tok), 1)
+    ).astype(F32)
+
+    def gate_step(v, carry):
+        turn = [
+            lax.dot_general(
+                eye, info[i, v], (((1,), (1,)), ((), ())),
+                precision=lax.Precision.HIGHEST, preferred_element_type=F32,
+            )
+            for i in range(2)
+        ]
+        index = lax.broadcasted_iota(jnp.int32, (tok, slots), 1).astype(F32)
+        gate[v] = (
+            jnp.where(index == turn[0][:, 0:1], turn[1][:, 0:1], 0.0)
+            + jnp.where(index == turn[0][:, 1:2], turn[1][:, 1:2], 0.0)
+        ).astype(BF)
+        return carry
+
+    for k in range(cols):
+        w2_copy(k).wait()
+
+    def r_copy(k, d):
+        return rem_copy(
+            comb_out.at[k, dp_peer(d)], comb_in.at[k, dp], rs.at[k, d], rr.at[k, d],
+            ex, dp_peer(d),
+        )
+
+    def out_step(s, carry):
+        @pl.when(s < cols)
+        def _():
+            def rows_step(b, c2):
+                at = pl.ds(pl.multiple_of(b * blk, 16), blk)
+                value = jnp.dot(hid[0, at], w2[s, 0:COL], preferred_element_type=F32)
+                for n in range(1, ffb):
+                    value = value + jnp.dot(
+                        hid[n, at], w2[s, n * COL : (n + 1) * COL], preferred_element_type=F32
+                    )
+                part_out[s, at] = value.astype(BF)
+                return c2
+
+            lax.fori_loop(0, 4, rows_step, 0)
+            for d in range(1, n_ex):
+                y_copy(s, d).start()
+            part_in[s, mine_seg] = part_out[s, mine_seg]
+
+        @pl.when(s == lag - 1)
+        def _():
+            lax.fori_loop(0, n_dp, gate_step, 0)
+
+        @pl.when(s >= lag)
+        def _():
+            k = s - lag
+            at = pl.ds(pl.multiple_of(k * COL, COL), COL)
+            for d in range(1, n_ex):
+                y_copy(k, d).wait_recv()
+
+            def comb_step(v, c2):
+                value = jnp.dot(gate[v], part_in[k], preferred_element_type=F32)
+
+                @pl.when(v == dp)
+                def _():
+                    res[:, at] += value
+
+                @pl.when(v != dp)
+                def _():
+                    comb_out[k, v] = value.astype(BF)
+
+                return c2
+
+            lax.fori_loop(0, n_dp, comb_step, 0)
+            for d in range(1, n_dp):
+                r_copy(k, d).start()
+
+        return carry
+
+    lax.fori_loop(0, cols + lag, out_step, 0)
+
+    def final_step(k, carry):
+        at = pl.ds(pl.multiple_of(k * COL, COL), COL)
+        value = res[:, at]
+        for d in range(1, n_dp):
+            r_copy(k, d).wait_recv()
+        for d in range(1, n_dp):
+            value = value + comb_in[k, dp_peer(d)].astype(F32)
+        o_ref[0, :, at] = value.astype(BF)
+        for d in range(1, n_dp):
+            z_copy(k, d).wait_send()
+            r_copy(k, d).wait_send()
+        for d in range(1, n_ex):
+            x_copy(k, d).wait_send()
+            y_copy(k, d).wait_send()
+        return carry
+
+    lax.fori_loop(0, cols, final_step, 0)
+    for d in range(1, n_dp):
+        info_copy(0, d, dp).wait_send()
+        info_copy(1, d, dp).wait_send()
+
+    @pl.when(dp < n_dp - 1)
+    def _():
+        up_copy().wait_send()
+
+    @pl.when(dp > 0)
+    def _():
+        down_copy().wait_send()
+
+
+def kernel_shards(n_ex, n_dp, cap, frames_in, conv_kernel, norm_gain, router, w_in, w_out, routes):
+    tok, width = frames_in.shape[1], frames_in.shape[2]
+    ff = w_in.shape[1]
+    cols, ffb = width // COL, ff // COL
+    slots = n_ex * n_dp * cap
+    dma = pltpu.SemaphoreType.DMA
+    vmem = pl.BlockSpec(memory_space=pltpu.VMEM)
+    hbm = pl.BlockSpec(memory_space=pl.ANY)
+    return pl.pallas_call(
+        functools.partial(moe_kernel, n_ex, n_dp, cap),
+        out_shape=jax.ShapeDtypeStruct(frames_in.shape, BF),
+        in_specs=[vmem] * 5 + [hbm] * 2,
+        out_specs=vmem,
+        scratch_shapes=[
+            pltpu.VMEM((tok + 2 * HALO, width), BF),
+            pltpu.VMEM((tok + 2 * HALO, LANE), F32),
+            pltpu.VMEM((tok, width), F32),
+            pltpu.VMEM((2, n_dp, 8, tok), F32),
+            pltpu.VMEM((slots, n_dp * tok), BF),
+            pltpu.VMEM((n_dp, tok, slots), BF),
+            pltpu.VMEM((cols, n_dp * tok, COL), BF),
+            pltpu.VMEM((cols, slots, COL), BF),
+            pltpu.VMEM((cols, slots, COL), BF),
+            pltpu.VMEM((ffb, slots, COL), F32),
+            pltpu.VMEM((ffb, slots, COL), BF),
+            pltpu.VMEM((cols, slots, COL), BF),
+            pltpu.VMEM((cols, slots, COL), BF),
+            pltpu.VMEM((cols, n_dp, tok, COL), BF),
+            pltpu.VMEM((cols, n_dp, tok, COL), BF),
+            pltpu.VMEM((cols, ff, COL), BF),
+            pltpu.VMEM((cols, ff, COL), BF),
+            pltpu.VMEM((n_ex, tok), F32),
+            dma((cols,)), dma((cols,)),
+            dma((2,)), dma((2,)),
+            dma((2, n_dp)), dma((2, n_dp)),
+            dma((cols, n_dp)), dma((cols, n_dp)),
+            dma((cols, n_ex)), dma((cols, n_ex)),
+            dma((cols, n_ex)), dma((cols, n_ex)),
+            dma((cols, n_dp)), dma((cols, n_dp)),
+        ],
+        compiler_params=pltpu.CompilerParams(
+            collective_id=0, has_side_effects=True, vmem_limit_bytes=56 * 2**20
+        ),
+    )(frames_in, conv_kernel, norm_gain[None], router.T, routes[0].T, w_in, w_out)
+
+
+def kernel_fits(n_ex, n_dp, cap, tok, width, ff, top_k, kernel_len):
+    seg = n_dp * cap
+    return (
+        n_ex == 8 and n_dp > 1 and top_k == 2 and tok % LANE == 0 and width % COL == 0
+        and ff % COL == 0 and seg % 16 == 0 and (n_ex * seg) % 64 == 0
+        and kernel_len <= 2 * HALO and kernel_len % 2 == 1
+        and 8 * n_ex * seg * (width + ff) + 4 * ff * width < 40 * 2**20
+    )
+
+
+def body(mesh, *args):
+    frames_in, conv_kernel, w_in, routes = args[0], args[1], args[4], args[6]
+    n_ex, n_dp = mesh.shape["expert"], mesh.shape["dp"]
+    tok, width, top_k = frames_in.shape[1], frames_in.shape[2], routes.shape[2]
+    cap = max(2, 9 * top_k * tok // (8 * n_ex))
+    if kernel_fits(n_ex, n_dp, cap, tok, width, w_in.shape[1], top_k, conv_kernel.shape[0]):
+        return kernel_shards(n_ex, n_dp, cap, *args)
+    return shards(*args)
+
+
 def solution(mesh):
     return jax.shard_map(
-        shards,
+        functools.partial(body, mesh),
         mesh=mesh,
         in_specs=(
             P("expert", "dp", None),

time: 282 us -> 123 us (0.44)
  waiting for transfers between devices: 211 us -> 0 us
  Pallas kernels: 0 us -> 119 us
  blocking collectives: 17.8 us -> 0 us
  other arithmetic: 16 us -> 0 us
  matrix products: 13.4 us -> 0 us
  starting transfers between devices: 11 us -> 0 us
  local copies, waits for them, and re-layouts: 8.78 us -> 3.05 us
    ppermute x5 -> x0, waiting for transfers between devices: 200 us -> none  [the longest x3 200 us: swapped(): return lax.ppermute(value, axis, pairs)]
    pallas_call x0 -> x1, Pallas kernels: none -> 119 us  [kernel_shards(): pl.pallas_call(functools.partial(moe_kernel, n_ex, n_dp, cap), out_shape=...]
    all_to_all x1 -> x0, blocking collectives: 17.8 us -> none  [shards(): lax.all_to_all(sent_normed, 'expert', split_axis=0, concat_axis=0, tiled=...]
    dot_general x5 -> x0, matrix products: 13.4 us -> none  [the longest x1 12 us: expert_block(): jnp.dot(hidden, stacked[1], preferred_element_type=jnp.float32)]
    all_to_all x1 -> x0, waiting for transfers between devices: 10.4 us -> none  [shards(): lax.all_to_all(expert_out, 'expert', split_axis=0, concat_axis=0, tiled=T...]
    convert_element_type x5 -> x0, other arithmetic: 10 us -> none  [the longest x1 5.23 us: shards(): (residual + jnp.sum(gating[:, :, None] * pulled_back, axis=1)).astype(jnp...]
    ppermute x5 -> x0, starting transfers between devices: 5.61 us -> none  [the longest x1 4.12 us: extended(): lax.ppermute(lax.slice_in_dim(block, 0, width, axis=dim), axis, backward)]
    all_to_all x1 -> x0, starting transfers between devices: 5.35 us -> none  [shards(): lax.all_to_all(expert_out, 'expert', split_axis=0, concat_axis=0, tiled=T...]
  transfers between devices with their start and end apart: 6 -> 0, of which waited for: 4 -> 0; matrix products, arithmetic and copies ran while one was open for 5% -> 0% of each run, Pallas kernels for 0% -> 0%
where the time goes in v1:
time: 123 us; the launch traced here: 122 us
  Pallas kernels  119 us (97%)
  local copies, waits for them, and re-layouts  3.05 us (2%)
    pallas_call x1, Pallas kernels, kernel_shards(): pl.pallas_call(functools.partial(moe_kernel, n_ex, n_dp, cap), out_shape=...  119 us

profile of v1, /device:TPU:29, one launch (start us, length us, event | category | flops | bytes accessed | tf_op | source)
XLA Modules:
  0.0 122.0 jit_solution(1327732836480139425)
XLA Ops:
  0.0 1.3 %broadcast_in_dim.3.gain_ref = bf16[1,1536]{1,0:T(2,128)(2,1)} reshape(bf16[1536]{0:T(1024)(128)(2,1)} %param.9) | data formatting | bytes 6144 | tf_op jit(solution)/shard_map/broadcast_in_dim | solution.py:528
  1.3 118.9 %shard_map.73 = bf16[1,128,1536]{2,1,0:T(8,128)(2,1)} custom-call(bf16[1,128,1536]{2,1,0:T(8,128)(2,1)} %x_ref.1, bf16[31,1536]{1,0:T(8,128)(2,1)} %ck_ref.1, bf16[1,1536]{1,0:T(2,128)(2,1)} %broadcast_in_dim.3.gain_ref, bf16[8,1536]{1,0:T(8,128)(2,1)} %bitcast.4, s32[2,128]{1,0:T(2,128)} %bitcast.5, bf16[1,768,1536]{2,1,0:T(8,128)(2,1)} %w_in_ref.1, ...), custom_call_target="tpu_custom_call" | custom-call | tf_op jit(solution)/shard_map/pallas_call | solution.py:493
  120.2 1.8 %copy.9 = bf16[1,128,1536]{2,1,0:T(8,128)(2,1)} copy(bf16[1,128,1536]{2,1,0:T(8,128)(2,1)} %shard_map.73) | data formatting | bytes 786432

commit v2 on v1

--- a/solution.py
+++ b/solution.py
@@ -113,6 +113,7 @@
 
 
 COL = 256
+FFB = 256
 LANE = 128
 HALO = 16
 BF = jnp.bfloat16
@@ -121,7 +122,8 @@
 
 
 def silu(v):
-    return v / (1.0 + jnp.exp(-v))
+    half = 0.5 * v
+    return half + half * jnp.tanh(half)
 
 
 def moe_kernel(
@@ -135,8 +137,9 @@
     tok, width = x_ref.shape[1], x_ref.shape[2]
     ff = w_in_ref.shape[1]
     cols = width // COL
-    ffb = ff // COL
-    margin = (ck_ref.shape[0] - 1) // 2
+    ffb = ff // FFB
+    taps_count = ck_ref.shape[0]
+    margin = (taps_count - 1) // 2
     seg = n_dp * cap
     slots = n_ex * seg
     ex = lax.axis_index("expert")
@@ -193,6 +196,26 @@
     ]
     info[0, dp] = jnp.where(rows8 == 0, targets[0], targets[1])
 
+    def conv_rows(first, count):
+        def step(c, carry):
+            at = pl.ds(pl.multiple_of(c * LANE, LANE), LANE)
+            span = count + 2 * HALO
+            xf[0:span, :] = xp[first : first + span, at].astype(F32)
+            taps = ck_ref[:, at].astype(F32)
+            conv = jnp.zeros((count, LANE), F32)
+            for r in range(8):
+                begin = HALO - margin + r
+                size = min(count + 24, span - begin)
+                shifted = xf[begin : begin + size, :]
+                for j in range(r, taps_count, 8):
+                    conv = conv + taps[j : j + 1, :] * shifted[j - r : j - r + count, :]
+            res[first : first + count, at] = xf[HALO : HALO + count, :] + silu(conv)
+            return carry
+
+        lax.fori_loop(0, width // LANE, step, 0)
+
+    conv_rows(HALO, tok - 2 * HALO)
+
     pl.semaphore_wait(barrier, n_dp - 1 + n_ex - 1)
 
     def up_copy():
@@ -239,19 +262,14 @@
     def _():
         down_copy().wait_recv()
 
-    def conv_step(c, total):
-        at = pl.ds(pl.multiple_of(c * LANE, LANE), LANE)
-        xf[...] = xp[:, at].astype(F32)
-        taps = ck_ref[:, at].astype(F32)
-        conv = jnp.zeros((tok, LANE), F32)
-        for j in range(ck_ref.shape[0]):
-            first = HALO - margin + j
-            conv = conv + taps[j : j + 1, :] * xf[first : first + tok, :]
-        value = xf[HALO : HALO + tok, :] + silu(conv)
-        res[:, at] = value
-        return total + jnp.sum(value * value, axis=1, keepdims=True)
-
-    total = lax.fori_loop(0, width // LANE, conv_step, jnp.zeros((tok, 1), F32))
+    conv_rows(0, HALO)
+    conv_rows(tok - HALO, HALO)
+
+    def square_step(k, total):
+        at = pl.ds(pl.multiple_of(k * COL, COL), COL)
+        return total + jnp.sum(res[:, at] * res[:, at], axis=1, keepdims=True)
+
+    total = lax.fori_loop(0, cols, square_step, jnp.zeros((tok, 1), F32))
     scale = lax.rsqrt(total * (1.0 / width) + 1e-6)
 
     own = pl.ds(pl.multiple_of(dp * tok, tok), tok)
@@ -262,13 +280,18 @@
         )
 
     logit[...] = jnp.zeros_like(logit)
+    ahead = 2
 
     def norm_step(k, carry):
         at = pl.ds(pl.multiple_of(k * COL, COL), COL)
         normed = (res[:, at] * scale * gain_ref[:, at].astype(F32)).astype(BF)
         frames[k, own] = normed
-        for d in range(1, n_dp):
-            z_copy(k, d).start()
+
+        @pl.when(k < ahead)
+        def _():
+            for d in range(1, n_dp):
+                z_copy(k, d).start()
+
         logit[...] += lax.dot_general(
             rout_ref[:, at], normed, (((1,), (1,)), ((), ())), preferred_element_type=F32
         )
@@ -323,6 +346,11 @@
             for d in range(1, n_dp):
                 z_copy(s, d).wait_recv()
 
+            @pl.when(s < cols - ahead)
+            def _():
+                for d in range(1, n_dp):
+                    z_copy(s + ahead, d).start()
+
             def rows_step(b, c2):
                 at = pl.ds(pl.multiple_of(b * blk, 16), blk)
                 rows_out[s, at] = jnp.dot(
@@ -342,7 +370,7 @@
                 x_copy(k, d).wait_recv()
 
             def ff_step(n, c2):
-                at = pl.ds(pl.multiple_of(n * COL, COL), COL)
+                at = pl.ds(pl.multiple_of(n * FFB, FFB), FFB)
                 got = lax.dot_general(
                     rows_in[k], w1[k, at], (((1,), (1,)), ((), ())), preferred_element_type=F32
                 )
@@ -407,10 +435,10 @@
         def _():
             def rows_step(b, c2):
                 at = pl.ds(pl.multiple_of(b * blk, 16), blk)
-                value = jnp.dot(hid[0, at], w2[s, 0:COL], preferred_element_type=F32)
+                value = jnp.dot(hid[0, at], w2[s, 0:FFB], preferred_element_type=F32)
                 for n in range(1, ffb):
                     value = value + jnp.dot(
-                        hid[n, at], w2[s, n * COL : (n + 1) * COL], preferred_element_type=F32
+                        hid[n, at], w2[s, n * FFB : (n + 1) * FFB], preferred_element_type=F32
                     )
                 part_out[s, at] = value.astype(BF)
                 return c2
@@ -485,7 +513,7 @@
 def kernel_shards(n_ex, n_dp, cap, frames_in, conv_kernel, norm_gain, router, w_in, w_out, routes):
     tok, width = frames_in.shape[1], frames_in.shape[2]
     ff = w_in.shape[1]
-    cols, ffb = width // COL, ff // COL
+    cols, ffb = width // COL, ff // FFB
     slots = n_ex * n_dp * cap
     dma = pltpu.SemaphoreType.DMA
     vmem = pl.BlockSpec(memory_space=pltpu.VMEM)
@@ -505,8 +533,8 @@
             pltpu.VMEM((cols, n_dp * tok, COL), BF),
             pltpu.VMEM((cols, slots, COL), BF),
             pltpu.VMEM((cols, slots, COL), BF),
-            pltpu.VMEM((ffb, slots, COL), F32),
-            pltpu.VMEM((ffb, slots, COL), BF),
+            pltpu.VMEM((ffb, slots, FFB), F32),
+            pltpu.VMEM((ffb, slots, FFB), BF),
             pltpu.VMEM((cols, slots, COL), BF),
             pltpu.VMEM((cols, slots, COL), BF),
             pltpu.VMEM((cols, n_dp, tok, COL), BF),
@@ -532,8 +560,8 @@
     seg = n_dp * cap
     return (
         n_ex == 8 and n_dp > 1 and top_k == 2 and tok % LANE == 0 and width % COL == 0
-        and ff % COL == 0 and seg % 16 == 0 and (n_ex * seg) % 64 == 0
-        and kernel_len <= 2 * HALO and kernel_len % 2 == 1
+        and ff % FFB == 0 and seg % 16 == 0 and (n_ex * seg) % 64 == 0
+        and kernel_len < 2 * HALO and kernel_len % 2 == 1
         and 8 * n_ex * seg * (width + ff) + 4 * ff * width < 40 * 2**20
     )
 

time: 123 us -> 118 us (0.959)
  Pallas kernels: 119 us -> 113 us
    pallas_call x1, Pallas kernels: 119 us -> 113 us  [kernel_shards(): pl.pallas_call(functools.partial(moe_kernel, n_ex, n_dp, cap), out_shape=...]
where the time goes in v2:
time: 118 us; the launch traced here: 116 us
  Pallas kernels  113 us (96%)
  local copies, waits for them, and re-layouts  3.05 us (3%)
    pallas_call x1, Pallas kernels, kernel_shards(): pl.pallas_call(functools.partial(moe_kernel, n_ex, n_dp, cap), out_shape=...  113 us

profile of v2, /device:TPU:29, one launch (start us, length us, event | category | flops | bytes accessed | tf_op | source)
XLA Modules:
  0.0 116.1 jit_solution(18313922998642576966)
XLA Ops:
  0.0 1.3 %broadcast_in_dim.3.gain_ref = bf16[1,1536]{1,0:T(2,128)(2,1)} reshape(bf16[1536]{0:T(1024)(128)(2,1)} %param.9) | data formatting | bytes 6144 | tf_op jit(solution)/shard_map/broadcast_in_dim | solution.py:556
  1.3 113.0 %shard_map.73 = bf16[1,128,1536]{2,1,0:T(8,128)(2,1)} custom-call(bf16[1,128,1536]{2,1,0:T(8,128)(2,1)} %x_ref.1, bf16[31,1536]{1,0:T(8,128)(2,1)} %ck_ref.1, bf16[1,1536]{1,0:T(2,128)(2,1)} %broadcast_in_dim.3.gain_ref, bf16[8,1536]{1,0:T(8,128)(2,1)} %bitcast.4, s32[2,128]{1,0:T(2,128)} %bitcast.5, bf16[1,768,1536]{2,1,0:T(8,128)(2,1)} %w_in_ref.1, ...), custom_call_target="tpu_custom_call" | custom-call | tf_op jit(solution)/shard_map/pallas_call | solution.py:521
  114.3 1.8 %copy.9 = bf16[1,128,1536]{2,1,0:T(8,128)(2,1)} copy(bf16[1,128,1536]{2,1,0:T(8,128)(2,1)} %shard_map.73) | data formatting | bytes 786432

commit v3 on v2

--- a/solution.py
+++ b/solution.py
@@ -112,7 +112,7 @@
     return combined[None]
 
 
-COL = 256
+COL = 128
 FFB = 256
 LANE = 128
 HALO = 16
@@ -280,7 +280,7 @@
         )
 
     logit[...] = jnp.zeros_like(logit)
-    ahead = 2
+    ahead = 4
 
     def norm_step(k, carry):
         at = pl.ds(pl.multiple_of(k * COL, COL), COL)
@@ -338,7 +338,7 @@
 
     for k in range(cols):
         w1_copy(k).wait()
-    lag = 2
+    lag = 3
 
     def in_step(s, carry):
         @pl.when(s < cols)

time: 118 us -> 119 us (level)
  the two profiles are of different devices: /device:TPU:29 before, /device:TPU:0 now
where the time goes in v3:
time: 119 us
  Pallas kernels  116 us (97%)
  local copies, waits for them, and re-layouts  3.05 us (3%)
    pallas_call x1, Pallas kernels, kernel_shards(): pl.pallas_call(functools.partial(moe_kernel, n_ex, n_dp, cap), out_shape=...  116 us

profile of v3, /device:TPU:0, one launch (start us, length us, event | category | flops | bytes accessed | tf_op | source)
XLA Modules:
  0.0 118.8 jit_solution(2440057524055452771)
XLA Ops:
  0.0 1.3 %broadcast_in_dim.3.gain_ref = bf16[1,1536]{1,0:T(2,128)(2,1)} reshape(bf16[1536]{0:T(1024)(128)(2,1)} %param.9) | data formatting | bytes 6144 | tf_op jit(solution)/shard_map/broadcast_in_dim | solution.py:556
  1.3 115.8 %shard_map.73 = bf16[1,128,1536]{2,1,0:T(8,128)(2,1)} custom-call(bf16[1,128,1536]{2,1,0:T(8,128)(2,1)} %x_ref.1, bf16[31,1536]{1,0:T(8,128)(2,1)} %ck_ref.1, bf16[1,1536]{1,0:T(2,128)(2,1)} %broadcast_in_dim.3.gain_ref, bf16[8,1536]{1,0:T(8,128)(2,1)} %bitcast.4, s32[2,128]{1,0:T(2,128)} %bitcast.5, bf16[1,768,1536]{2,1,0:T(8,128)(2,1)} %w_in_ref.1, ...), custom_call_target="tpu_custom_call" | custom-call | tf_op jit(solution)/shard_map/pallas_call | solution.py:521
  117.1 1.8 %copy.9 = bf16[1,128,1536]{2,1,0:T(8,128)(2,1)} copy(bf16[1,128,1536]{2,1,0:T(8,128)(2,1)} %shard_map.73) | data formatting | bytes 786432

commit v4 on v2

--- a/solution.py
+++ b/solution.py
@@ -126,13 +126,19 @@
     return half + half * jnp.tanh(half)
 
 
+def pad_of(cap):
+    return -(-cap // 16) * 16
+
+
 def moe_kernel(
     n_ex, n_dp, cap,
     x_ref, ck_ref, gain_ref, rout_ref, routes_ref, w_in_ref, w_out_ref,
     o_ref,
     xp, xf, res, info, place, gate, frames, rows_out, rows_in, acc, hid, part_out, part_in,
     comb_out, comb_in, w1, w2, logit,
+    info2, place2, gate2, spread, gather, rows2_out, rows2_in, z2_out, z2_in, y2_out, y2_in,
     w1_sem, w2_sem, halo_s, halo_r, info_s, info_r, zs, zr, xs, xr, ys, yr, rs, rr,
+    x2s, x2r, zxs, zxr, z2s, z2r, y2s, y2r,
 ):
     tok, width = x_ref.shape[1], x_ref.shape[2]
     ff = w_in_ref.shape[1]
@@ -145,6 +151,8 @@
     ex = lax.axis_index("expert")
     dp = lax.axis_index("dp")
     blk = slots // 4
+    pad = pad_of(cap)
+    last = cols - 1
 
     def dp_peer(d):
         return lax.rem(dp + d, n_dp)
@@ -188,12 +196,27 @@
     count = jnp.dot((hot[0] + hot[1]).astype(BF), before, preferred_element_type=F32)
     counts = [count, count + hot[0]]
     rows8 = lax.broadcasted_iota(jnp.int32, (8, tok), 0)
-    targets = [
-        routes_ref[k : k + 1, :].astype(F32) * seg
-        + (dp * cap).astype(F32)
-        + jnp.sum(counts[k] * hot[k], axis=0, keepdims=True)
-        for k in range(2)
-    ]
+    slot = [jnp.sum(counts[k] * hot[k], axis=0, keepdims=True) for k in range(2)]
+    named = [routes_ref[k : k + 1, :].astype(F32) for k in range(2)]
+    targets = [named[k] * seg + (dp * cap).astype(F32) + slot[k] for k in range(2)]
+    targets2 = [named[k] * pad + slot[k] for k in range(2)]
+    info2[...] = jnp.where(rows8 == 0, targets2[0], targets2[1])
+    index2 = lax.broadcasted_iota(jnp.int32, (n_ex * pad, tok), 0).astype(F32)
+    place2[...] = (
+        jnp.where(index2 == targets2[0], 1.0, 0.0) + jnp.where(index2 == targets2[1], 1.0, 0.0)
+    ).astype(BF)
+
+    def spread_of(shape, seg_dim):
+        i = lax.broadcasted_iota(jnp.int32, shape, seg_dim)
+        j = lax.broadcasted_iota(jnp.int32, shape, 1 - seg_dim)
+        hits = jnp.zeros(shape, F32)
+        for v in range(n_dp):
+            inside = (i >= v * cap) & (i < (v + 1) * cap)
+            hits = hits + jnp.where(inside & (j - i == v * (pad - cap)), 1.0, 0.0)
+        return hits.astype(BF)
+
+    spread[...] = spread_of((seg, n_dp * pad), 0)
+    gather[...] = spread_of((n_dp * pad, seg), 1)
     info[0, dp] = jnp.where(rows8 == 0, targets[0], targets[1])
 
     def conv_rows(first, count):
@@ -298,6 +321,39 @@
         return carry
 
     lax.fori_loop(0, cols, norm_step, 0)
+    mine_pad = pl.ds(pl.multiple_of(ex * pad, 16), pad)
+
+    def pad_at(e):
+        return pl.ds(pl.multiple_of(e * pad, 16), pad)
+
+    def x2_copy(d):
+        return rem_copy(
+            rows2_out.at[pad_at(ex_peer(d))], rows2_in.at[dp, mine_pad],
+            x2s.at[d], x2r.at[d], ex_peer(d), dp,
+        )
+
+    def zx_copy(d):
+        return rem_copy(
+            rows2_in.at[dp], rows2_in.at[dp], zxs.at[d], zxr.at[d], ex, dp_peer(d)
+        )
+
+    def z2_copy(d):
+        return rem_copy(
+            z2_out.at[dp_peer(d)], z2_in.at[dp], z2s.at[d], z2r.at[d], ex, dp_peer(d)
+        )
+
+    def y2_copy(d):
+        return rem_copy(
+            y2_out.at[pad_at(ex_peer(d))], y2_in.at[mine_pad],
+            y2s.at[d], y2r.at[d], ex_peer(d), dp,
+        )
+
+    rows2_out[...] = jnp.dot(
+        place2[...], frames[last, own], preferred_element_type=F32
+    ).astype(BF)
+    for d in range(1, n_ex):
+        x2_copy(d).start()
+    rows2_in[dp, mine_pad] = rows2_out[mine_pad, :]
     gating = [
         1.0 / (1.0 + jnp.exp(-jnp.sum(hot[k] * logit[...], axis=0, keepdims=True)))
         for k in range(2)
@@ -340,16 +396,42 @@
         w1_copy(k).wait()
     lag = 2
 
+    def first_matmul(k):
+        def ff_step(n, c2):
+            at = pl.ds(pl.multiple_of(n * FFB, FFB), FFB)
+            got = lax.dot_general(
+                rows_in[k], w1[k, at], (((1,), (1,)), ((), ())), preferred_element_type=F32
+            )
+
+            @pl.when(k == 0)
+            def _():
+                acc[n] = got
+
+            @pl.when(k > 0)
+            def _():
+                acc[n] += got
+
+            return c2
+
+        lax.fori_loop(0, ffb, ff_step, 0)
+
     def in_step(s, carry):
-        @pl.when(s < cols)
+        @pl.when(s < last)
         def _():
             for d in range(1, n_dp):
                 z_copy(s, d).wait_recv()
 
-            @pl.when(s < cols - ahead)
+            @pl.when(s < last - ahead)
             def _():
                 for d in range(1, n_dp):
                     z_copy(s + ahead, d).start()
+
+            @pl.when(s == last - ahead - 1)
+            def _():
+                for d in range(1, n_ex):
+                    x2_copy(d).wait_recv()
+                for d in range(1, n_dp):
+                    zx_copy(d).start()
 
             def rows_step(b, c2):
                 at = pl.ds(pl.multiple_of(b * blk, 16), blk)
@@ -365,31 +447,25 @@
 
         @pl.when(s >= lag)
         def _():
-            k = s - lag
             for d in range(1, n_ex):
-                x_copy(k, d).wait_recv()
-
-            def ff_step(n, c2):
-                at = pl.ds(pl.multiple_of(n * FFB, FFB), FFB)
-                got = lax.dot_general(
-                    rows_in[k], w1[k, at], (((1,), (1,)), ((), ())), preferred_element_type=F32
-                )
-
-                @pl.when(k == 0)
-                def _():
-                    acc[n] = got
-
-                @pl.when(k > 0)
-                def _():
-                    acc[n] += got
-
-                return c2
-
-            lax.fori_loop(0, ffb, ff_step, 0)
-
-        return carry
-
-    lax.fori_loop(0, cols + lag, in_step, 0)
+                x_copy(s - lag, d).wait_recv()
+            first_matmul(s - lag)
+
+        return carry
+
+    lax.fori_loop(0, last + lag, in_step, 0)
+    for d in range(1, n_dp):
+        zx_copy(d).wait_recv()
+
+    def spread_step(u, carry):
+        got = jnp.concatenate([rows2_in[v, pad_at(u)] for v in range(n_dp)], axis=0)
+        rows_in[last, seg_of(u)] = jnp.dot(
+            spread[...], got, preferred_element_type=F32
+        ).astype(BF)
+        return carry
+
+    lax.fori_loop(0, n_ex, spread_step, 0)
+    first_matmul(jnp.int32(last))
 
     def silu_step(b, carry):
         at = pl.ds(pl.multiple_of(b * blk, 16), blk)
@@ -430,27 +506,69 @@
             ex, dp_peer(d),
         )
 
+    def second_matmul(k):
+        def rows_step(b, c2):
+            at = pl.ds(pl.multiple_of(b * blk, 16), blk)
+            value = jnp.dot(hid[0, at], w2[k, 0:FFB], preferred_element_type=F32)
+            for n in range(1, ffb):
+                value = value + jnp.dot(
+                    hid[n, at], w2[k, n * FFB : (n + 1) * FFB], preferred_element_type=F32
+                )
+            part_out[k, at] = value.astype(BF)
+            return c2
+
+        lax.fori_loop(0, 4, rows_step, 0)
+
+    def gather_step(u, carry):
+        got = jnp.dot(
+            gather[...], part_out[last, seg_of(u)], preferred_element_type=F32
+        ).astype(BF)
+        for v in range(n_dp):
+            z2_out[v, pad_at(u)] = got[v * pad : (v + 1) * pad]
+        return carry
+
     def out_step(s, carry):
-        @pl.when(s < cols)
+        @pl.when(s < last)
         def _():
-            def rows_step(b, c2):
-                at = pl.ds(pl.multiple_of(b * blk, 16), blk)
-                value = jnp.dot(hid[0, at], w2[s, 0:FFB], preferred_element_type=F32)
-                for n in range(1, ffb):
-                    value = value + jnp.dot(
-                        hid[n, at], w2[s, n * FFB : (n + 1) * FFB], preferred_element_type=F32
-                    )
-                part_out[s, at] = value.astype(BF)
-                return c2
-
-            lax.fori_loop(0, 4, rows_step, 0)
+            second_matmul(s)
             for d in range(1, n_ex):
                 y_copy(s, d).start()
             part_in[s, mine_seg] = part_out[s, mine_seg]
 
+        @pl.when(s == 0)
+        def _():
+            second_matmul(jnp.int32(last))
+            lax.fori_loop(0, n_ex, gather_step, 0)
+            for d in range(1, n_dp):
+                z2_copy(d).start()
+
+        @pl.when(s == last - 1)
+        def _():
+            total2 = z2_out[dp].astype(F32)
+            for d in range(1, n_dp):
+                z2_copy(d).wait_recv()
+            for d in range(1, n_dp):
+                total2 = total2 + z2_in[dp_peer(d)].astype(F32)
+            y2_out[...] = total2.astype(BF)
+            for d in range(1, n_ex):
+                y2_copy(d).start()
+            y2_in[mine_pad, :] = y2_out[mine_pad, :]
+
         @pl.when(s == lag - 1)
         def _():
             lax.fori_loop(0, n_dp, gate_step, 0)
+            turn = [
+                lax.dot_general(
+                    eye, mat, (((1,), (1,)), ((), ())),
+                    precision=lax.Precision.HIGHEST, preferred_element_type=F32,
+                )
+                for mat in (info2[...], info[1, dp])
+            ]
+            across = lax.broadcasted_iota(jnp.int32, (tok, n_ex * pad), 1).astype(F32)
+            gate2[...] = (
+                jnp.where(across == turn[0][:, 0:1], turn[1][:, 0:1], 0.0)
+                + jnp.where(across == turn[0][:, 1:2], turn[1][:, 1:2], 0.0)
+            ).astype(BF)
 
         @pl.when(s >= lag)
         def _():
@@ -478,7 +596,13 @@
 
         return carry
 
-    lax.fori_loop(0, cols + lag, out_step, 0)
+    lax.fori_loop(0, last + lag, out_step, 0)
+    for d in range(1, n_ex):
+        y2_copy(d).wait_recv()
+    ending = slice(last * COL, width)
+    o_ref[0, :, ending] = (
+        res[:, ending] + jnp.dot(gate2[...], y2_in[...], preferred_element_type=F32)
+    ).astype(BF)
 
     def final_step(k, carry):
         at = pl.ds(pl.multiple_of(k * COL, COL), COL)
@@ -496,7 +620,13 @@
             y_copy(k, d).wait_send()
         return carry
 
-    lax.fori_loop(0, cols, final_step, 0)
+    lax.fori_loop(0, last, final_step, 0)
+    for d in range(1, n_dp):
+        zx_copy(d).wait_send()
+        z2_copy(d).wait_send()
+    for d in range(1, n_ex):
+        x2_copy(d).wait_send()
+        y2_copy(d).wait_send()
     for d in range(1, n_dp):
         info_copy(0, d, dp).wait_send()
         info_copy(1, d, dp).wait_send()
@@ -515,6 +645,8 @@
     ff = w_in.shape[1]
     cols, ffb = width // COL, ff // FFB
     slots = n_ex * n_dp * cap
+    pad = pad_of(cap)
+    wide = n_ex * pad
     dma = pltpu.SemaphoreType.DMA
     vmem = pl.BlockSpec(memory_space=pltpu.VMEM)
     hbm = pl.BlockSpec(memory_space=pl.ANY)
@@ -542,6 +674,17 @@
             pltpu.VMEM((cols, ff, COL), BF),
             pltpu.VMEM((cols, ff, COL), BF),
             pltpu.VMEM((n_ex, tok), F32),
+            pltpu.VMEM((8, tok), F32),
+            pltpu.VMEM((wide, tok), BF),
+            pltpu.VMEM((tok, wide), BF),
+            pltpu.VMEM((n_dp * cap, n_dp * pad), BF),
+            pltpu.VMEM((n_dp * pad, n_dp * cap), BF),
+            pltpu.VMEM((wide, COL), BF),
+            pltpu.VMEM((n_dp, wide, COL), BF),
+            pltpu.VMEM((n_dp, wide, COL), BF),
+            pltpu.VMEM((n_dp, wide, COL), BF),
+            pltpu.VMEM((wide, COL), BF),
+            pltpu.VMEM((wide, COL), BF),
             dma((cols,)), dma((cols,)),
             dma((2,)), dma((2,)),
             dma((2, n_dp)), dma((2, n_dp)),
@@ -549,6 +692,8 @@
             dma((cols, n_ex)), dma((cols, n_ex)),
             dma((cols, n_ex)), dma((cols, n_ex)),
             dma((cols, n_dp)), dma((cols, n_dp)),
+            dma((n_ex,)), dma((n_ex,)), dma((n_dp,)), dma((n_dp,)),
+            dma((n_dp,)), dma((n_dp,)), dma((n_ex,)), dma((n_ex,)),
         ],
         compiler_params=pltpu.CompilerParams(
             collective_id=0, has_side_effects=True, vmem_limit_bytes=56 * 2**20
@@ -559,7 +704,7 @@
 def kernel_fits(n_ex, n_dp, cap, tok, width, ff, top_k, kernel_len):
     seg = n_dp * cap
     return (
-        n_ex == 8 and n_dp > 1 and top_k == 2 and tok % LANE == 0 and width % COL == 0
+        n_ex == 8 and n_dp > 1 and top_k == 2 and tok % LANE == 0 and width % COL == 0 and width >= 4 * COL
         and ff % FFB == 0 and seg % 16 == 0 and (n_ex * seg) % 64 == 0
         and kernel_len < 2 * HALO and kernel_len % 2 == 1
         and 8 * n_ex * seg * (width + ff) + 4 * ff * width < 40 * 2**20

time: 118 us -> 118 us (level)
  no operation moved by 1% of the time
where the time goes in v4:
time: 118 us; the launch traced here: 116 us
  Pallas kernels  113 us (96%)
  local copies, waits for them, and re-layouts  3.05 us (3%)
    pallas_call x1, Pallas kernels, kernel_shards(): pl.pallas_call(functools.partial(moe_kernel, n_ex, n_dp, cap), out_shape=...  113 us

profile of v4, /device:TPU:29, one launch (start us, length us, event | category | flops | bytes accessed | tf_op | source)
XLA Modules:
  0.0 115.6 jit_solution(17310080422851438908)
XLA Ops:
  0.0 1.3 %broadcast_in_dim.3.gain_ref = bf16[1,1536]{1,0:T(2,128)(2,1)} reshape(bf16[1536]{0:T(1024)(128)(2,1)} %param.9) | data formatting | bytes 6144 | tf_op jit(solution)/shard_map/broadcast_in_dim | solution.py:701
  1.3 112.6 %shard_map.73 = bf16[1,128,1536]{2,1,0:T(8,128)(2,1)} custom-call(bf16[1,128,1536]{2,1,0:T(8,128)(2,1)} %x_ref.1, bf16[31,1536]{1,0:T(8,128)(2,1)} %ck_ref.1, bf16[1,1536]{1,0:T(2,128)(2,1)} %broadcast_in_dim.3.gain_ref, bf16[8,1536]{1,0:T(8,128)(2,1)} %bitcast.4, s32[2,128]{1,0:T(2,128)} %bitcast.5, bf16[1,768,1536]{2,1,0:T(8,128)(2,1)} %w_in_ref.1, ...), custom_call_target="tpu_custom_call" | custom-call | tf_op jit(solution)/shard_map/pallas_call | solution.py:653
  113.9 1.8 %copy.9 = bf16[1,128,1536]{2,1,0:T(8,128)(2,1)} copy(bf16[1,128,1536]{2,1,0:T(8,128)(2,1)} %shard_map.73) | data formatting | bytes 786432

commit v5 on v4

--- a/solution.py
+++ b/solution.py
@@ -138,7 +138,7 @@
     comb_out, comb_in, w1, w2, logit,
     info2, place2, gate2, spread, gather, rows2_out, rows2_in, z2_out, z2_in, y2_out, y2_in,
     w1_sem, w2_sem, halo_s, halo_r, info_s, info_r, zs, zr, xs, xr, ys, yr, rs, rr,
-    x2s, x2r, zxs, zxr, z2s, z2r, y2s, y2r,
+    x2s, x2r, zxs, zxr, z2s, z2r, y2s, y2r, added, fs, ads, adr,
 ):
     tok, width = x_ref.shape[1], x_ref.shape[2]
     ff = w_in_ref.shape[1]
@@ -165,6 +165,18 @@
             src_ref=src, dst_ref=dst, send_sem=ssem, recv_sem=rsem,
             device_id=(e, v), device_id_type=MESH,
         )
+
+    relay = n_dp == 4
+    inner = jnp.logical_and(dp > 0, dp < n_dp - 1)
+    outer = jnp.logical_not(inner)
+
+    def unless_far(relayed, d, run):
+        if relay and d == n_dp - 1:
+            pl.when(jnp.logical_not(jnp.logical_and(relayed, dp == 0)))(run)
+        elif relay and d == 1:
+            pl.when(jnp.logical_not(jnp.logical_and(relayed, dp == n_dp - 1)))(run)
+        else:
+            run()
 
     barrier = pltpu.get_barrier_semaphore()
     for d in range(1, n_dp):
@@ -302,6 +314,17 @@
             frames.at[k, own], frames.at[k, own], zs.at[k, d], zr.at[k, d], ex, dp_peer(d)
         )
 
+    def z_start(k):
+        for d in range(1, n_dp):
+            unless_far(k >= 1, d, z_copy(k, d).start)
+
+    def z_forward(k):
+        block = pl.ds(pl.multiple_of((2 - dp) * 3 * tok, tok), tok)
+        return rem_copy(
+            frames.at[k, block], frames.at[k, block],
+            fs.at[k], zr.at[k, 2 * dp - 1], ex, (dp - 1) * 3,
+        )
+
     logit[...] = jnp.zeros_like(logit)
     ahead = 2
 
@@ -312,8 +335,7 @@
 
         @pl.when(k < ahead)
         def _():
-            for d in range(1, n_dp):
-                z_copy(k, d).start()
+            z_start(k)
 
         logit[...] += lax.dot_general(
             rout_ref[:, at], normed, (((1,), (1,)), ((), ())), preferred_element_type=F32
@@ -421,10 +443,15 @@
             for d in range(1, n_dp):
                 z_copy(s, d).wait_recv()
 
+            if relay:
+
+                @pl.when(jnp.logical_and(inner, s >= 1))
+                def _():
+                    z_forward(s).start()
+
             @pl.when(s < last - ahead)
             def _():
-                for d in range(1, n_dp):
-                    z_copy(s + ahead, d).start()
+                z_start(s + ahead)
 
             @pl.when(s == last - ahead - 1)
             def _():
@@ -505,6 +532,26 @@
             comb_out.at[k, dp_peer(d)], comb_in.at[k, dp], rs.at[k, d], rr.at[k, d],
             ex, dp_peer(d),
         )
+
+    def add_copy(k):
+        return rem_copy(
+            comb_out.at[k, 3 - dp], added.at[k], ads.at[k], adr.at[k], ex, 1 + dp // 3
+        )
+
+    def r_start(k):
+        for d in range(1, n_dp):
+            if relay and d == 2:
+                pl.when(jnp.logical_or(outer, k >= last - 1))(r_copy(k, d).start)
+            else:
+                unless_far(k < last - 1, d, r_copy(k, d).start)
+        if relay:
+            pl.when(jnp.logical_and(outer, k < last - 1))(add_copy(k).start)
+
+    def r_late(k):
+        add_copy(k).wait_recv()
+        far = 3 * (2 - dp)
+        comb_out[k, far] = (comb_out[k, far].astype(F32) + added[k].astype(F32)).astype(BF)
+        r_copy(k, 2).start()
 
     def second_matmul(k):
         def rows_step(b, c2):
@@ -570,6 +617,12 @@
                 + jnp.where(across == turn[0][:, 1:2], turn[1][:, 1:2], 0.0)
             ).astype(BF)
 
+        if relay:
+
+            @pl.when(jnp.logical_and(inner, s > lag))
+            def _():
+                r_late(s - lag - 1)
+
         @pl.when(s >= lag)
         def _():
             k = s - lag
@@ -591,8 +644,7 @@
                 return c2
 
             lax.fori_loop(0, n_dp, comb_step, 0)
-            for d in range(1, n_dp):
-                r_copy(k, d).start()
+            r_start(k)
 
         return carry
 
@@ -606,15 +658,28 @@
 
     def final_step(k, carry):
         at = pl.ds(pl.multiple_of(k * COL, COL), COL)
-        value = res[:, at]
+
+        def take(d):
+            def run():
+                r_copy(k, d).wait_recv()
+                res[:, at] += comb_in[k, lax.rem(dp + n_dp - d, n_dp)].astype(F32)
+
+            if relay and d == n_dp - 1:
+                pl.when(jnp.logical_not(jnp.logical_and(k < last - 1, dp == n_dp - 1)))(run)
+            elif relay and d == 1:
+                pl.when(jnp.logical_not(jnp.logical_and(k < last - 1, dp == 0)))(run)
+            else:
+                run()
+
         for d in range(1, n_dp):
-            r_copy(k, d).wait_recv()
+            take(d)
+        o_ref[0, :, at] = res[:, at].astype(BF)
         for d in range(1, n_dp):
-            value = value + comb_in[k, dp_peer(d)].astype(F32)
-        o_ref[0, :, at] = value.astype(BF)
-        for d in range(1, n_dp):
-            z_copy(k, d).wait_send()
-            r_copy(k, d).wait_send()
+            unless_far(k >= 1, d, z_copy(k, d).wait_send)
+            unless_far(k < last - 1, d, r_copy(k, d).wait_send)
+        if relay:
+            pl.when(jnp.logical_and(inner, k >= 1))(z_forward(k).wait_send)
+            pl.when(jnp.logical_and(outer, k < last - 1))(add_copy(k).wait_send)
         for d in range(1, n_ex):
             x_copy(k, d).wait_send()
             y_copy(k, d).wait_send()
@@ -694,6 +759,8 @@
             dma((cols, n_dp)), dma((cols, n_dp)),
             dma((n_ex,)), dma((n_ex,)), dma((n_dp,)), dma((n_dp,)),
             dma((n_dp,)), dma((n_dp,)), dma((n_ex,)), dma((n_ex,)),
+            pltpu.VMEM((cols, tok, COL), BF),
+            dma((cols,)), dma((cols,)), dma((cols,)),
         ],
         compiler_params=pltpu.CompilerParams(
             collective_id=0, has_side_effects=True, vmem_limit_bytes=56 * 2**20

time: 118 us -> 114 us (0.966); the launches traced: 116 us -> 114 us
  Pallas kernels: 113 us -> 111 us
    pallas_call x1, Pallas kernels: 113 us -> 111 us  [kernel_shards(): pl.pallas_call(functools.partial(moe_kernel, n_ex, n_dp, cap), out_shape=...]
where the time goes in v5:
time: 114 us
  Pallas kernels  111 us (97%)
  local copies, waits for them, and re-layouts  3.05 us (3%)
    pallas_call x1, Pallas kernels, kernel_shards(): pl.pallas_call(functools.partial(moe_kernel, n_ex, n_dp, cap), out_shape=...  111 us

profile of v5, /device:TPU:29, one launch (start us, length us, event | category | flops | bytes accessed | tf_op | source)
XLA Modules:
  0.0 114.2 jit_solution(11929310434501688509)
XLA Ops:
  0.0 1.3 %broadcast_in_dim.3.gain_ref = bf16[1,1536]{1,0:T(2,128)(2,1)} reshape(bf16[1536]{0:T(1024)(128)(2,1)} %param.9) | data formatting | bytes 6144 | tf_op jit(solution)/shard_map/broadcast_in_dim | solution.py:768
  1.3 111.1 %shard_map.73 = bf16[1,128,1536]{2,1,0:T(8,128)(2,1)} custom-call(bf16[1,128,1536]{2,1,0:T(8,128)(2,1)} %x_ref.1, bf16[31,1536]{1,0:T(8,128)(2,1)} %ck_ref.1, bf16[1,1536]{1,0:T(2,128)(2,1)} %broadcast_in_dim.3.gain_ref, bf16[8,1536]{1,0:T(8,128)(2,1)} %bitcast.4, s32[2,128]{1,0:T(2,128)} %bitcast.5, bf16[1,768,1536]{2,1,0:T(8,128)(2,1)} %w_in_ref.1, ...), custom_call_target="tpu_custom_call" | custom-call | tf_op jit(solution)/shard_map/pallas_call | solution.py:718
  112.4 1.8 %copy.9 = bf16[1,128,1536]{2,1,0:T(8,128)(2,1)} copy(bf16[1,128,1536]{2,1,0:T(8,128)(2,1)} %shard_map.73) | data formatting | bytes 786432

commit v6 on v5

--- a/solution.py
+++ b/solution.py
@@ -151,6 +151,7 @@
     ex = lax.axis_index("expert")
     dp = lax.axis_index("dp")
     blk = slots // 4
+    half = slots // 2
     pad = pad_of(cap)
     last = cols - 1
 
@@ -359,6 +360,13 @@
             rows2_in.at[dp], rows2_in.at[dp], zxs.at[d], zxr.at[d], ex, dp_peer(d)
         )
 
+    def zx_forward():
+        block = (2 - dp) * 3
+        return rem_copy(
+            rows2_in.at[block], rows2_in.at[block],
+            fs.at[last], zxr.at[2 * dp - 1], ex, (dp - 1) * 3,
+        )
+
     def z2_copy(d):
         return rem_copy(
             z2_out.at[dp_peer(d)], z2_in.at[dp], z2s.at[d], z2r.at[d], ex, dp_peer(d)
@@ -458,19 +466,26 @@
                 for d in range(1, n_ex):
                     x2_copy(d).wait_recv()
                 for d in range(1, n_dp):
-                    zx_copy(d).start()
+                    unless_far(True, d, zx_copy(d).start)
 
             def rows_step(b, c2):
-                at = pl.ds(pl.multiple_of(b * blk, 16), blk)
+                at = pl.ds(pl.multiple_of(b * half, 16), half)
                 rows_out[s, at] = jnp.dot(
                     place[at, :], frames[s], preferred_element_type=F32
                 ).astype(BF)
                 return c2
 
-            lax.fori_loop(0, 4, rows_step, 0)
+            lax.fori_loop(0, 2, rows_step, 0)
             for d in range(1, n_ex):
                 x_copy(s, d).start()
             rows_in[s, mine_seg] = rows_out[s, mine_seg]
+
+        if relay:
+
+            @pl.when(jnp.logical_and(inner, s == last + lag - 1))
+            def _():
+                zx_copy(2).wait_recv()
+                zx_forward().start()
 
         @pl.when(s >= lag)
         def _():
@@ -482,7 +497,10 @@
 
     lax.fori_loop(0, last + lag, in_step, 0)
     for d in range(1, n_dp):
-        zx_copy(d).wait_recv()
+        if relay and d == 2:
+            pl.when(outer)(zx_copy(d).wait_recv)
+        else:
+            zx_copy(d).wait_recv()
 
     def spread_step(u, carry):
         got = jnp.concatenate([rows2_in[v, pad_at(u)] for v in range(n_dp)], axis=0)
@@ -518,7 +536,7 @@
             for i in range(2)
         ]
         index = lax.broadcasted_iota(jnp.int32, (tok, slots), 1).astype(F32)
-        gate[v] = (
+        gate[pl.ds(pl.multiple_of(v * tok, tok), tok)] = (
             jnp.where(index == turn[0][:, 0:1], turn[1][:, 0:1], 0.0)
             + jnp.where(index == turn[0][:, 1:2], turn[1][:, 1:2], 0.0)
         ).astype(BF)
@@ -555,7 +573,7 @@
 
     def second_matmul(k):
         def rows_step(b, c2):
-            at = pl.ds(pl.multiple_of(b * blk, 16), blk)
+            at = pl.ds(pl.multiple_of(b * half, 16), half)
             value = jnp.dot(hid[0, at], w2[k, 0:FFB], preferred_element_type=F32)
             for n in range(1, ffb):
                 value = value + jnp.dot(
@@ -564,7 +582,7 @@
             part_out[k, at] = value.astype(BF)
             return c2
 
-        lax.fori_loop(0, 4, rows_step, 0)
+        lax.fori_loop(0, 2, rows_step, 0)
 
     def gather_step(u, carry):
         got = jnp.dot(
@@ -630,20 +648,18 @@
             for d in range(1, n_ex):
                 y_copy(k, d).wait_recv()
 
-            def comb_step(v, c2):
-                value = jnp.dot(gate[v], part_in[k], preferred_element_type=F32)
-
-                @pl.when(v == dp)
-                def _():
+            sums = jnp.dot(gate[...], part_in[k], preferred_element_type=F32)
+            for v in range(n_dp):
+                value = sums[v * tok : (v + 1) * tok]
+
+                @pl.when(dp == v)
+                def _(value=value):
                     res[:, at] += value
 
-                @pl.when(v != dp)
-                def _():
+                @pl.when(dp != v)
+                def _(v=v, value=value):
                     comb_out[k, v] = value.astype(BF)
 
-                return c2
-
-            lax.fori_loop(0, n_dp, comb_step, 0)
             r_start(k)
 
         return carry
@@ -687,8 +703,10 @@
 
     lax.fori_loop(0, last, final_step, 0)
     for d in range(1, n_dp):
-        zx_copy(d).wait_send()
+        unless_far(True, d, zx_copy(d).wait_send)
         z2_copy(d).wait_send()
+    if relay:
+        pl.when(inner)(zx_forward().wait_send)
     for d in range(1, n_ex):
         x2_copy(d).wait_send()
         y2_copy(d).wait_send()
@@ -726,7 +744,7 @@
             pltpu.VMEM((tok, width), F32),
             pltpu.VMEM((2, n_dp, 8, tok), F32),
             pltpu.VMEM((slots, n_dp * tok), BF),
-            pltpu.VMEM((n_dp, tok, slots), BF),
+            pltpu.VMEM((n_dp * tok, slots), BF),
             pltpu.VMEM((cols, n_dp * tok, COL), BF),
             pltpu.VMEM((cols, slots, COL), BF),
             pltpu.VMEM((cols, slots, COL), BF),

time: 114 us -> 109 us (0.956)
  Pallas kernels: 111 us -> 106 us
    pallas_call x1, Pallas kernels: 111 us -> 106 us  [kernel_shards(): pl.pallas_call(functools.partial(moe_kernel, n_ex, n_dp, cap), out_shape=...]
where the time goes in v6:
time: 109 us
  Pallas kernels  106 us (97%)
  local copies, waits for them, and re-layouts  3.05 us (3%)
    pallas_call x1, Pallas kernels, kernel_shards(): pl.pallas_call(functools.partial(moe_kernel, n_ex, n_dp, cap), out_shape=...  106 us

profile of v6, /device:TPU:29, one launch (start us, length us, event | category | flops | bytes accessed | tf_op | source)
XLA Modules:
  0.0 108.7 jit_solution(8142754787252425322)
XLA Ops:
  0.0 1.3 %broadcast_in_dim.3.gain_ref = bf16[1,1536]{1,0:T(2,128)(2,1)} reshape(bf16[1536]{0:T(1024)(128)(2,1)} %param.9) | data formatting | bytes 6144 | tf_op jit(solution)/shard_map/broadcast_in_dim | solution.py:786
  1.3 105.6 %shard_map.73 = bf16[1,128,1536]{2,1,0:T(8,128)(2,1)} custom-call(bf16[1,128,1536]{2,1,0:T(8,128)(2,1)} %x_ref.1, bf16[31,1536]{1,0:T(8,128)(2,1)} %ck_ref.1, bf16[1,1536]{1,0:T(2,128)(2,1)} %broadcast_in_dim.3.gain_ref, bf16[8,1536]{1,0:T(8,128)(2,1)} %bitcast.4, s32[2,128]{1,0:T(2,128)} %bitcast.5, bf16[1,768,1536]{2,1,0:T(8,128)(2,1)} %w_in_ref.1, ...), custom_call_target="tpu_custom_call" | custom-call | tf_op jit(solution)/shard_map/pallas_call | solution.py:736
  106.9 1.8 %copy.9 = bf16[1,128,1536]{2,1,0:T(8,128)(2,1)} copy(bf16[1,128,1536]{2,1,0:T(8,128)(2,1)} %shard_map.73) | data formatting | bytes 786432

commit v7 on v6

--- a/solution.py
+++ b/solution.py
@@ -468,14 +468,9 @@
                 for d in range(1, n_dp):
                     unless_far(True, d, zx_copy(d).start)
 
-            def rows_step(b, c2):
-                at = pl.ds(pl.multiple_of(b * half, 16), half)
-                rows_out[s, at] = jnp.dot(
-                    place[at, :], frames[s], preferred_element_type=F32
-                ).astype(BF)
-                return c2
-
-            lax.fori_loop(0, 2, rows_step, 0)
+            rows_out[s] = jnp.dot(
+                place[...], frames[s], preferred_element_type=F32
+            ).astype(BF)
             for d in range(1, n_ex):
                 x_copy(s, d).start()
             rows_in[s, mine_seg] = rows_out[s, mine_seg]
@@ -515,7 +510,7 @@
     def silu_step(b, carry):
         at = pl.ds(pl.multiple_of(b * blk, 16), blk)
         for n in range(ffb):
-            hid[n, at] = silu(acc[n, at]).astype(BF)
+            hid[at, n * FFB : (n + 1) * FFB] = silu(acc[n, at]).astype(BF)
         return carry
 
     lax.fori_loop(0, 4, silu_step, 0)
@@ -574,11 +569,7 @@
     def second_matmul(k):
         def rows_step(b, c2):
             at = pl.ds(pl.multiple_of(b * half, 16), half)
-            value = jnp.dot(hid[0, at], w2[k, 0:FFB], preferred_element_type=F32)
-            for n in range(1, ffb):
-                value = value + jnp.dot(
-                    hid[n, at], w2[k, n * FFB : (n + 1) * FFB], preferred_element_type=F32
-                )
+            value = jnp.dot(hid[at, :], w2[k], preferred_element_type=F32)
             part_out[k, at] = value.astype(BF)
             return c2
 
@@ -749,7 +740,7 @@
             pltpu.VMEM((cols, slots, COL), BF),
             pltpu.VMEM((cols, slots, COL), BF),
             pltpu.VMEM((ffb, slots, FFB), F32),
-            pltpu.VMEM((ffb, slots, FFB), BF),
+            pltpu.VMEM((slots, ff), BF),
             pltpu.VMEM((cols, slots, COL), BF),
             pltpu.VMEM((cols, slots, COL), BF),
             pltpu.VMEM((cols, n_dp, tok, COL), BF),

time: 109 us -> 109 us (level)
  no operation moved by 1% of the time
where the time goes in v7:
time: 109 us
  Pallas kernels  105 us (96%)
  local copies, waits for them, and re-layouts  3.05 us (3%)
    pallas_call x1, Pallas kernels, kernel_shards(): pl.pallas_call(functools.partial(moe_kernel, n_ex, n_dp, cap), out_shape=...  105 us

profile of v7, /device:TPU:29, one launch (start us, length us, event | category | flops | bytes accessed | tf_op | source)
XLA Modules:
  0.0 108.5 jit_solution(8234334112732040481)
XLA Ops:
  0.0 1.3 %broadcast_in_dim.3.gain_ref = bf16[1,1536]{1,0:T(2,128)(2,1)} reshape(bf16[1536]{0:T(1024)(128)(2,1)} %param.9) | data formatting | bytes 6144 | tf_op jit(solution)/shard_map/broadcast_in_dim | solution.py:777
  1.3 105.5 %shard_map.73 = bf16[1,128,1536]{2,1,0:T(8,128)(2,1)} custom-call(bf16[1,128,1536]{2,1,0:T(8,128)(2,1)} %x_ref.1, bf16[31,1536]{1,0:T(8,128)(2,1)} %ck_ref.1, bf16[1,1536]{1,0:T(2,128)(2,1)} %broadcast_in_dim.3.gain_ref, bf16[8,1536]{1,0:T(8,128)(2,1)} %bitcast.4, s32[2,128]{1,0:T(2,128)} %bitcast.5, bf16[1,768,1536]{2,1,0:T(8,128)(2,1)} %w_in_ref.1, ...), custom_call_target="tpu_custom_call" | custom-call | tf_op jit(solution)/shard_map/pallas_call | solution.py:727
  106.8 1.8 %copy.9 = bf16[1,128,1536]{2,1,0:T(8,128)(2,1)} copy(bf16[1,128,1536]{2,1,0:T(8,128)(2,1)} %shard_map.73) | data formatting | bytes 786432

commit v8 on v7

--- a/solution.py
+++ b/solution.py
@@ -327,7 +327,7 @@
         )
 
     logit[...] = jnp.zeros_like(logit)
-    ahead = 2
+    ahead = 3
 
     def norm_step(k, carry):
         at = pl.ds(pl.multiple_of(k * COL, COL), COL)
@@ -504,7 +504,7 @@
         ).astype(BF)
         return carry
 
-    lax.fori_loop(0, n_ex, spread_step, 0)
+    lax.fori_loop(0, n_ex, spread_step, 0, unroll=True)
     first_matmul(jnp.int32(last))
 
     def silu_step(b, carry):
@@ -594,7 +594,7 @@
         @pl.when(s == 0)
         def _():
             second_matmul(jnp.int32(last))
-            lax.fori_loop(0, n_ex, gather_step, 0)
+            lax.fori_loop(0, n_ex, gather_step, 0, unroll=True)
             for d in range(1, n_dp):
                 z2_copy(d).start()
 

time: 109 us -> 110 us (level)
  Pallas kernels: 105 us -> 107 us
    pallas_call x1, Pallas kernels: 105 us -> 107 us  [kernel_shards(): pl.pallas_call(functools.partial(moe_kernel, n_ex, n_dp, cap), out_shape=...]
where the time goes in v8:
time: 110 us
  Pallas kernels  107 us (97%)
  local copies, waits for them, and re-layouts  3.05 us (3%)
    pallas_call x1, Pallas kernels, kernel_shards(): pl.pallas_call(functools.partial(moe_kernel, n_ex, n_dp, cap), out_shape=...  107 us

profile of v8, /device:TPU:29, one launch (start us, length us, event | category | flops | bytes accessed | tf_op | source)
XLA Modules:
  0.0 110.1 jit_solution(11041762752803085649)
XLA Ops:
  0.0 1.3 %broadcast_in_dim.3.gain_ref = bf16[1,1536]{1,0:T(2,128)(2,1)} reshape(bf16[1536]{0:T(1024)(128)(2,1)} %param.9) | data formatting | bytes 6144 | tf_op jit(solution)/shard_map/broadcast_in_dim | solution.py:777
  1.3 107.0 %shard_map.73 = bf16[1,128,1536]{2,1,0:T(8,128)(2,1)} custom-call(bf16[1,128,1536]{2,1,0:T(8,128)(2,1)} %x_ref.1, bf16[31,1536]{1,0:T(8,128)(2,1)} %ck_ref.1, bf16[1,1536]{1,0:T(2,128)(2,1)} %broadcast_in_dim.3.gain_ref, bf16[8,1536]{1,0:T(8,128)(2,1)} %bitcast.4, s32[2,128]{1,0:T(2,128)} %bitcast.5, bf16[1,768,1536]{2,1,0:T(8,128)(2,1)} %w_in_ref.1, ...), custom_call_target="tpu_custom_call" | custom-call | tf_op jit(solution)/shard_map/pallas_call | solution.py:727
  108.3 1.8 %copy.9 = bf16[1,128,1536]{2,1,0:T(8,128)(2,1)} copy(bf16[1,128,1536]{2,1,0:T(8,128)(2,1)} %shard_map.73) | data formatting | bytes 786432
